TPU v7x, 128 devices: a whole 4x4x4 slice. The times are simulated.
128 devices in a mesh: owner: 32 (over y, z, core), split: 4 (over x).
Axes of the slice: x: 4, y: 4, z: 4, core: 2. Of those that a mesh axis runs over, the one named last changes fastest.
Arguments:
- embeddings: bfloat16 [131072, 768], P(('owner', 'split')), may hold values from -6 to 6
- cluster: int32 [131072], P(('owner', 'split')), may hold values from 0 to 31, as said below
- order: int32 [131072], P(('owner', 'split')), may hold values from 0 to 131071, each once
Outputs:
- max_cosine: float32 [131072], P(('owner', 'split'))
Inputs may be any that keep to these rules, and one draw needn't show every extreme that they name: Cluster c belongs to owner c. Of one device's rows at most 64 lie in clusters of one owner and at most 64 in one cluster; on every device some owner receives exactly 64 and each of its clusters exactly 64. `order`: all ranks are distinct.
All inputs are finite; a program needn't handle non-finite values.
Results may differ from a plain program's by a relative error of at most 0.0013.
Values may be sent and summed in bfloat16 or wider, within the bound.
No kernel may reach another device: no remote copies, remote signals or barrier semaphores. Data moves between devices by JAX's collectives and lax.ppermute only.
A program may use at most 64 MiB of HBM per device.

v0:
```python
import functools

import jax
import jax.numpy as jnp
from jax import lax
from jax.experimental import pallas as pl
from jax.experimental.pallas import tpu as pltpu
from jax.sharding import PartitionSpec as P

D = 768
LANES = 128
BLOCKS = D // LANES
SLOTS = 16
DATA = SLOTS * BLOCKS
MSG = DATA + 8
CLUSTERS = 32
PEERS = 128
ROWS = PEERS * SLOTS
GROUPS = ROWS // LANES
GROUP = LANES // SLOTS
LONE = 256
FACTS = 16
FAR = float(2**20)
BLOCK = 512
AXES = ("owner", "split")
VMEM = 56 * 2**20


def slot_of(index):
    return (index & 31) >> 1


def pair_of(cluster, index):
    return ((cluster >> 1) * 2 + (index & 1)) * 2 + (cluster & 1)


def my_core():
    return lax.axis_index("owner") % 2


def my_late():
    return lax.axis_index("split") % 2


def iota(shape, axis):
    return lax.broadcasted_iota(jnp.int32, shape, axis)


def ones_where(mask):
    return jnp.where(mask, 1.0, 0.0).astype(jnp.bfloat16)


def dot_nt(a, b):
    return lax.dot_general(a, b, (((1,), (1,)), ((), ())), preferred_element_type=jnp.float32)


def dot_nn(a, b):
    return lax.dot_general(a, b, (((1,), (0,)), ((), ())), preferred_element_type=jnp.float32)


def thirds(x):
    first = x.astype(jnp.bfloat16)
    left = x - first.astype(jnp.float32)
    second = left.astype(jnp.bfloat16)
    return first, second, (left - second.astype(jnp.float32)).astype(jnp.bfloat16)


def pack_kernel(emb_ref, cluster_ref, order_ref, out_ref, index_ref, unit_ref, at_ref, some_ref, some_at_ref, late_ref, meta_ref, past_ref):
    step = pl.program_id(0)
    rows = emb_ref.shape[0]
    pairs = PEERS // 2
    tile = pairs // pl.num_programs(0)

    @pl.when(step == 0)
    def _():
        values = emb_ref[...].astype(jnp.float32)
        total = jnp.sum(values * values, axis=1, keepdims=True)
        unit_ref[...] = (values * lax.rsqrt(total + 1e-06)).astype(jnp.bfloat16)
        cluster = cluster_ref[...]
        rank = order_ref[...]
        hit = iota((CLUSTERS, rows), 0) == cluster
        hits = ones_where(hit)
        upper = ones_where(iota((LANES, LANES), 0) <= iota((LANES, LANES), 1))
        blocks = rows // LANES
        ahead = dot_nn(hits, ones_where(iota((rows, LANES), 0) >> 7 < iota((rows, LANES), 1)))
        counted = jnp.concatenate(
            [
                dot_nn(hits[:, b * LANES:(b + 1) * LANES], upper) + ahead[:, b:b + 1]
                for b in range(blocks)
            ],
            axis=1,
        )
        counts = jnp.broadcast_to(ahead[:, blocks:blocks + 1], (CLUSTERS, LANES))
        below = ones_where(iota((CLUSTERS, CLUSTERS), 1) < iota((CLUSTERS, CLUSTERS), 0))
        over = jnp.maximum(counts - 32.0, 0.0)
        begin = dot_nn(below, over.astype(jnp.bfloat16))

        def of_row(x):
            return jnp.sum(jnp.where(hit, x, 0.0), axis=0, keepdims=True).astype(jnp.int32)

        index = of_row(counted) - 1
        count = of_row(counts[:, :1])
        index_ref[0:1, :] = index
        index_ref[1:2, :] = count
        slot = slot_of(index)
        pair = pair_of(cluster, index)
        first = index < 32
        last = index + 32 >= count
        at_ref[0:1, :] = jnp.where(first, pair * SLOTS + slot, -1)
        at_ref[1:2, :] = jnp.where(first, -1, of_row(begin[:, :1]) + index - 32)
        at_ref[2:3, :] = pair
        at_ref[3:4, :] = slot
        past_ref[0] = jnp.sum(over[:, :1]).astype(jnp.int32)
        sends = iota((pairs, rows), 0) == pair
        sends = jnp.concatenate(
            [jnp.where(sends & first, 1.0, 0.0), jnp.where(sends & last, 1.0, 0.0)], axis=0
        )
        high = ((rank >> 9) + 1).astype(jnp.float32)
        low = ((rank & 511) - 256).astype(jnp.float32)
        at_slot = ones_where((iota((LANES, rows), 0) & (SLOTS - 1)) == slot)
        meta_ref[0] = dot_nt((sends * high).astype(jnp.bfloat16), at_slot)
        meta_ref[1] = dot_nt((sends * low).astype(jnp.bfloat16), at_slot)
        spread = jnp.where(iota((CLUSTERS, LANES), 0) == iota((CLUSTERS, LANES), 1), counts, 0.0)
        meta_ref[2] = jnp.broadcast_to(jnp.sum(spread, axis=0, keepdims=True), (PEERS, LANES))
        place = iota((PEERS, CLUSTERS), 0) & (pairs - 1)
        theirs = ones_where((place >> 2) * 2 + (place & 1) == iota((PEERS, CLUSTERS), 1))
        meta_ref[3] = dot_nn(theirs, counts.astype(jnp.bfloat16))

    def bring(chunk):
        start = chunk * LANES
        chosen = ones_where(iota((LANES, rows), 0) + start == at_ref[1:2, :])
        some_ref[pl.ds(start, LANES), :] = dot_nn(chosen, unit_ref[...]).astype(jnp.bfloat16)
        places = jnp.where(iota((8, rows), 0) == 0, at_ref[2:3, :] + 1, at_ref[3:4, :])
        place = dot_nt(places.astype(jnp.float32).astype(jnp.bfloat16), chosen)
        target = ((place[0:1, :] - 1.0) * SLOTS + place[1:2, :]).astype(jnp.int32)
        some_at_ref[chunk] = jnp.broadcast_to(jnp.where(place[0:1, :] > 0.5, target, -1), (8, LANES))

    @pl.when(step == 0)
    def _():
        bring(0)

    size = tile * SLOTS
    chosen = ones_where(iota((size, rows), 0) + step * size == at_ref[0:1, :])
    early = dot_nn(chosen, unit_ref[...])

    def spread_some(chunk, late):
        here = iota((size, LANES), 0) + step * size == some_at_ref[chunk][0:1, :]
        some = dot_nn(ones_where(here), some_ref[chunk * LANES:(chunk + 1) * LANES, :])
        taken = jnp.sum(jnp.where(here, 1.0, 0.0), axis=1, keepdims=True)
        return jnp.where(taken > 0.5, some, late)

    late = spread_some(0, early)
    start = pl.multiple_of(step * tile, tile)

    def put(half, rows_at):
        packed = rows_at.astype(jnp.bfloat16)
        for block in range(BLOCKS):
            out_ref[:, half, block * SLOTS:(block + 1) * SLOTS, :] = packed[
                :, block * LANES:(block + 1) * LANES
            ].reshape(tile, SLOTS, LANES)

    put(0, early)
    put(1, late)
    late_ref[...] = late
    at = iota((tile, 8, LANES), 1)
    for half in range(2):
        meta = jnp.zeros((tile, 8, LANES), jnp.float32)
        for i in range(4):
            meta = jnp.where(at == i, meta_ref[i, pl.ds(start + half * pairs, tile), :][:, None, :], meta)
        out_ref[:, half, DATA:MSG, :] = meta.astype(jnp.bfloat16)

    @pl.when(past_ref[0] > LANES)
    def _():
        for chunk in range(1, rows // LANES // 2):
            bring(chunk)
            late_ref[...] = spread_some(chunk, late_ref[...])
        put(1, late_ref[...])


def pack(embeddings, cluster, order):
    rows = embeddings.shape[0]
    steps = 2
    message, index = pl.pallas_call(
        pack_kernel,
        grid=(steps,),
        in_specs=[
            pl.BlockSpec((rows, D), lambda i: (0, 0)),
            pl.BlockSpec((1, rows), lambda i: (0, 0)),
            pl.BlockSpec((1, rows), lambda i: (0, 0)),
        ],
        out_specs=[
            pl.BlockSpec((PEERS // 2 // steps, 2, MSG, LANES), lambda i: (i, 0, 0, 0)),
            pl.BlockSpec((2, rows), lambda i: (0, 0)),
        ],
        out_shape=[
            jax.ShapeDtypeStruct((PEERS // 2, 2, MSG, LANES), jnp.bfloat16),
            jax.ShapeDtypeStruct((2, rows), jnp.int32),
        ],
        scratch_shapes=[
            pltpu.VMEM((rows, D), jnp.bfloat16),
            pltpu.VMEM((8, rows), jnp.int32),
            pltpu.VMEM((rows // 2, D), jnp.bfloat16),
            pltpu.VMEM((rows // LANES // 2, 8, LANES), jnp.int32),
            pltpu.VMEM((rows // steps, D), jnp.float32),
            pltpu.VMEM((4, PEERS, LANES), jnp.float32),
            pltpu.SMEM((1,), jnp.int32),
        ],
        compiler_params=pltpu.CompilerParams(vmem_limit_bytes=VMEM),
        name="pack",
    )(embeddings, cluster.reshape(1, rows), order.reshape(1, rows))
    return message.reshape(PEERS, MSG, LANES), index


def units_of(ref, start, count):
    first, peers = start // SLOTS, count // SLOTS
    return jnp.concatenate(
        [
            ref[first:first + peers, b * SLOTS:(b + 1) * SLOTS, :].reshape(count, LANES)
            for b in range(BLOCKS)
        ],
        axis=1,
    )


def meta_of(ref):
    meta = ref[:, DATA:MSG, :].astype(jnp.float32).reshape(GROUPS, GROUP, 8, LANES)
    mine = iota((1, GROUP, 8, LANES), 3) >> 4 == iota((1, GROUP, 8, LANES), 1)
    return jnp.sum(jnp.where(mine, meta, 0.0), axis=1), meta


def rank_from(high, low):
    return jnp.where(high > 0.5, high * 512.0 + low, FAR)


def ranks_of(ref):
    held, _ = meta_of(ref)
    return rank_from(held[:, 0:1, :], held[:, 1:2, :])


def as_row(blocks):
    return jnp.concatenate([blocks[b] for b in range(GROUPS)], axis=1)


def as_columns(blocks, out_ref):
    for b in range(GROUPS):
        out_ref[b * LANES:(b + 1) * LANES, :] = jnp.broadcast_to(blocks[b], (LANES, LANES)).T


def row_of_best(ref):
    return jnp.concatenate(
        [
            jnp.max(ref[b * LANES:(b + 1) * LANES, :].T, axis=0, keepdims=True)
            for b in range(ref.shape[0] // LANES)
        ],
        axis=1,
    )


def lone_kernel(round_ref, msg_ref, out_ref, most_ref):
    core = my_core()
    first = 0 if round_ref is None else round_ref[0] * LONE
    held, meta = meta_of(msg_ref)
    high, low, count = (held[:, i:i + 1, :] for i in (0, 1, 3))
    half = jnp.floor((jnp.maximum(meta[:, :, 2, :] - 32.0, 0.0) + 1.0) * 0.5)
    most = jnp.sum(jnp.sum(half, axis=0), axis=0, keepdims=True)
    most_ref[...] = jnp.max(most, axis=1, keepdims=True).astype(jnp.int32)

    index = (2 * (iota((GROUPS, 1, LANES), 2) & 15) + core + 32).astype(jnp.float32)
    lone = jnp.where(index < count, 1.0, 0.0)
    lone = jnp.concatenate([lone[b] for b in range(GROUPS)], axis=0).astype(jnp.bfloat16)
    upper = ones_where(iota((LANES, LANES), 0) <= iota((LANES, LANES), 1))
    counted = dot_nn(lone, upper)
    whole = jnp.broadcast_to(counted[:, LANES - 1:LANES], (GROUPS, LANES)).astype(jnp.bfloat16)
    below = ones_where(iota((GROUPS, GROUPS), 1) < iota((GROUPS, GROUPS), 0))
    position = (counted + dot_nn(below, whole)).astype(jnp.int32) - 1 - first
    position = jnp.where(lone > 0.5, position, -1)
    position = jnp.concatenate([position[b:b + 1, :] for b in range(GROUPS)], axis=1)
    chosen = ones_where(iota((LONE, ROWS), 0) == position)
    out_ref[:LONE, :] = dot_nn(chosen, units_of(msg_ref, 0, ROWS)).astype(jnp.bfloat16)
    at = iota((FACTS, ROWS), 0)
    row = iota((FACTS, ROWS), 1)
    facts = jnp.where(at == 2, row >> 4, jnp.where(at == 3, row & 15, 0)).astype(jnp.float32)
    facts = jnp.where(at == 0, as_row(high), jnp.where(at == 1, as_row(low), facts))
    facts = dot_nt(facts.astype(jnp.bfloat16), chosen).astype(jnp.bfloat16)
    out_ref[LONE:, :LONE] = facts
    out_ref[LONE:, LONE:] = jnp.zeros((FACTS, D - LONE), jnp.bfloat16)


def gather_lone(msg, round_at=None):
    some = [] if round_at is None else [round_at.reshape(1)]
    return pl.pallas_call(
        lone_kernel if some else functools.partial(lone_kernel, None),
        in_specs=[pl.BlockSpec(memory_space=pltpu.SMEM)] * len(some)
        + [pl.BlockSpec(memory_space=pltpu.VMEM)],
        out_specs=[pl.BlockSpec(memory_space=pltpu.VMEM)] * 2,
        out_shape=[
            jax.ShapeDtypeStruct((LONE + FACTS, D), jnp.bfloat16),
            jax.ShapeDtypeStruct((1, 1), jnp.int32),
        ],
        compiler_params=pltpu.CompilerParams(vmem_limit_bytes=VMEM),
        name="lone",
    )(*some, msg)


def narrow_rows(x):
    best = x[:, :LANES]
    for b in range(1, x.shape[1] // LANES):
        best = jnp.maximum(best, x[:, b * LANES:(b + 1) * LANES])
    return best


def narrow_cols(x):
    return jnp.max(x.reshape(x.shape[0] // 8, 8, x.shape[1]), axis=0)


def wide(column, count):
    return jnp.concatenate([column] * (count // LANES), axis=1)


def span(i):
    return slice(i * BLOCK, (i + 1) * BLOCK)


def lone_facts(ref):
    facts = ref[LONE:, :LONE].astype(jnp.float32)
    peer = jnp.where(facts[0:1, :] > 0.5, facts[2:3, :].astype(jnp.int32), -1)
    return rank_from(facts[0:1, :], facts[1:2, :]), peer, facts[3:4, :].astype(jnp.int32)


def pairs_kernel(own_ref, other_ref, lone_ref, beside_ref, out_ref, found_ref, rank_ref, rows_ref, cols_ref, some_ref):
    core, late = my_core(), my_late()
    own_ranks = ranks_of(own_ref)
    as_columns(own_ranks, rank_ref)
    count = ROWS // BLOCK
    rows_ref[...] = jnp.full((ROWS, LANES), -1.0, jnp.float32)
    cols_ref[...] = jnp.full((8, ROWS), -1.0, jnp.float32)

    def score(right_ref, row, i, j, both):
        scores = dot_nt(units_of(own_ref, i * BLOCK, BLOCK), units_of(right_ref, j * BLOCK, BLOCK))
        earlier = row[:, span(j)] < wide(rank_ref[span(i), :], BLOCK)
        kept = narrow_rows(jnp.where(earlier, scores, -1.0))
        rows_ref[span(i), :] = jnp.maximum(rows_ref[span(i), :], kept)
        if both:
            kept = narrow_cols(jnp.where(earlier, -1.0, scores))
            cols_ref[:, span(j)] = jnp.maximum(cols_ref[:, span(j)], kept)

    @pl.when(late == 0)
    def _():
        row = as_row(own_ranks)
        for i in range(count):
            for j in range(i, count):
                score(own_ref, row, i, j, i != j)
        some_ref[...] = beside_ref[...]

    def across(firsts, seconds):
        row = as_row(ranks_of(other_ref))
        for i in firsts:
            for j in seconds:
                score(other_ref, row, i, j, True)
        some_ref[...] = lone_ref[...]

    @pl.when((late == 1) & (core == 0))
    def _():
        across(range(count), range(count // 2))

    @pl.when((late == 1) & (core == 1))
    def _():
        across(range(count // 2, count), range(count))

    some = some_ref[:LONE, :]
    some_rank, _, _ = lone_facts(some_ref)
    found = jnp.full((8, LONE), -1.0, jnp.float32)
    for i in range(count):
        scores = dot_nt(units_of(own_ref, i * BLOCK, BLOCK), some)
        rank = wide(rank_ref[span(i), :], LONE)
        kept = narrow_rows(jnp.where(some_rank < rank, scores, -1.0))
        rows_ref[span(i), :] = jnp.maximum(rows_ref[span(i), :], kept)
        found = jnp.maximum(found, narrow_cols(jnp.where(rank < some_rank, scores, -1.0)))
    found_ref[...] = jnp.max(found, axis=0, keepdims=True)
    own_best = row_of_best(rows_ref)
    cols_best = jnp.max(cols_ref[...], axis=0, keepdims=True)
    out_ref[0:1, :] = jnp.where(late == 0, jnp.maximum(own_best, cols_best), own_best)
    out_ref[1:2, :] = jnp.where(late == 0, -1.0, cols_best)


def score_pairs(own, other, lone, beside):
    return pl.pallas_call(
        pairs_kernel,
        in_specs=[pl.BlockSpec(memory_space=pltpu.VMEM)] * 4,
        out_specs=[pl.BlockSpec(memory_space=pltpu.VMEM)] * 2,
        out_shape=[
            jax.ShapeDtypeStruct((2, ROWS), jnp.float32),
            jax.ShapeDtypeStruct((1, LONE), jnp.float32),
        ],
        scratch_shapes=[
            pltpu.VMEM((ROWS, LANES), jnp.float32),
            pltpu.VMEM((ROWS, LANES), jnp.float32),
            pltpu.VMEM((8, ROWS), jnp.float32),
            pltpu.VMEM((LONE + FACTS, D), jnp.bfloat16),
        ],
        compiler_params=pltpu.CompilerParams(vmem_limit_bytes=VMEM),
        name="pairs",
    )(own, other, lone, beside)


def as_table(row):
    mine = iota((GROUP, LANES), 1) >> 4 == iota((GROUP, LANES), 0)
    parts = []
    for b in range(GROUPS):
        part = jnp.where(mine, row[:, b * LANES:(b + 1) * LANES], 0.0)
        for shift in (64, 32, 16):
            part = part + pltpu.roll(part, shift, 1)
        parts.append(part)
    return jnp.concatenate(parts, axis=0)


def finish_kernel(lone_ref, beside_ref, late_ref, best_ref, found_ref, out_ref):
    core, late = my_core(), my_late()
    late_rank, late_peer, late_slot = lone_facts(late_ref)
    late_column = jnp.broadcast_to(late_rank, (LANES, LONE))
    late_column = jnp.concatenate(
        [late_column[:, b * LANES:(b + 1) * LANES].T for b in range(LONE // LANES)], axis=0
    )
    late_column = wide(late_column, LONE)
    late_best = jnp.full((LONE, LANES), -1.0, jnp.float32)
    found = []
    for ref in (lone_ref, beside_ref):
        rank, peer, slot = lone_facts(ref)
        scores = dot_nt(late_ref[:LONE, :], ref[:LONE, :])
        late_best = jnp.maximum(late_best, narrow_rows(jnp.where(rank < late_column, scores, -1.0)))
        best = jnp.max(jnp.where(late_column < rank, scores, -1.0), axis=0, keepdims=True)
        found.append((best, peer, slot))
    late_best = jnp.concatenate(
        [
            jnp.max(late_best[b * LANES:(b + 1) * LANES, :].T, axis=0, keepdims=True)
            for b in range(LONE // LANES)
        ],
        axis=1,
    )
    earlier_found = found_ref[...]
    own = jnp.maximum(found[0][0], jnp.where(late == 1, earlier_found, -1.0))
    other = jnp.maximum(found[1][0], jnp.where(late == 0, earlier_found, -1.0))
    best = jnp.concatenate([own, other, late_best], axis=1)
    peer = jnp.concatenate([found[0][1], found[1][1], late_peer], axis=1)
    slot = jnp.concatenate(
        [found[0][2] + SLOTS * core, found[1][2] + SLOTS * (1 - core), late_slot + 2 * SLOTS], axis=1
    )
    at_peer = ones_where(iota((PEERS, 3 * LONE), 0) == peer)
    at_slot = iota((LANES, 3 * LONE), 0) == slot
    placed = dot_nt(at_peer, ones_where(at_slot))
    value = jnp.where(at_slot, best, 0.0)
    value = sum(dot_nt(at_peer, part) for part in thirds(value))
    table = jnp.where(placed > 0.5, value, -1.0)
    lane = iota((PEERS, LANES), 1)
    rest = jnp.where(
        lane >> 4 == core,
        as_table(best_ref[0:1, :]),
        jnp.where(lane < 2 * SLOTS, as_table(best_ref[1:2, :]), -1.0),
    )
    out_ref[...] = jnp.maximum(table, rest)


def finish(lone, beside, late_rows, best, found):
    return pl.pallas_call(
        finish_kernel,
        in_specs=[pl.BlockSpec(memory_space=pltpu.VMEM)] * 5,
        out_specs=pl.BlockSpec(memory_space=pltpu.VMEM),
        out_shape=jax.ShapeDtypeStruct((PEERS, LANES), jnp.float32),
        compiler_params=pltpu.CompilerParams(vmem_limit_bytes=VMEM),
        name="finish",
    )(lone, beside, late_rows, best, found)


def reply_kernel(table_ref, cluster_ref, index_ref, out_ref):
    cluster = cluster_ref[...]
    index = index_ref[0:1, :]
    count = index_ref[1:2, :]
    rows = cluster.shape[1]
    table = table_ref[...]
    lane = iota((PEERS, LANES), 1)
    early = jnp.maximum(table, pltpu.roll(table, PEERS - 4, 0))
    beside = jnp.where(
        lane < SLOTS,
        pltpu.roll(table, LANES - 2 * SLOTS, 1),
        pltpu.roll(pltpu.roll(table, PEERS - 4, 0), LANES - SLOTS, 1),
    )
    late = jnp.maximum(pltpu.roll(early, PEERS - 1, 0), beside)
    both = jnp.concatenate([early.T[:2 * SLOTS, :], late.T[:2 * SLOTS, :]], axis=0)
    chosen = ones_where(iota((PEERS, rows), 0) == pair_of(cluster, jnp.zeros_like(index)) * 2)
    picked = sum(dot_nn(part, chosen) for part in thirds(both))
    at = (index & 1) * SLOTS + slot_of(index)
    here = iota((4 * SLOTS, rows), 0)
    here = ((here == at) & (index < 32)) | ((here == at + 2 * SLOTS) & (index + 32 >= count))
    out_ref[...] = jnp.max(jnp.where(here, picked, -1.0), axis=0, keepdims=True)


def read_reply(table, cluster, index):
    rows = cluster.shape[0]
    best = pl.pallas_call(
        reply_kernel,
        in_specs=[pl.BlockSpec(memory_space=pltpu.VMEM)] * 3,
        out_specs=pl.BlockSpec(memory_space=pltpu.VMEM),
        out_shape=jax.ShapeDtypeStruct((1, rows), jnp.float32),
        compiler_params=pltpu.CompilerParams(vmem_limit_bytes=VMEM),
        name="reply",
    )(table, cluster.reshape(1, rows), index)
    return best.reshape(rows)


def device(chip, core, column):
    return (chip * 2 + core) * 4 + column


SWAP = [
    (device(chip, core, column), device(chip, 1 - core, column))
    for chip in range(16)
    for core in range(2)
    for column in range(4)
]
OTHER_CHIP = [
    (device(chip, core, column), device(chip, core, column ^ 1))
    for chip in range(16)
    for core in range(2)
    for column in range(4)
]


def shards(embeddings, cluster, order):
    message, index = pack(embeddings, cluster, order)
    own = lax.all_to_all(message, AXES, split_axis=0, concat_axis=0, tiled=True)
    other = lax.ppermute(own, AXES, SWAP)

    def score(lone, far):
        beside = lax.ppermute(lone, AXES, SWAP)
        far = lax.ppermute(far, AXES, OTHER_CHIP)
        best, found = score_pairs(own, other, lone, beside)
        return finish(lone, beside, far, best, found)

    lone, most = gather_lone(own)
    table = score(lone, lone)
    rounds = (most[0, 0] + LONE - 1) // LONE

    def one_round(state):
        at, table = state
        lone, _ = gather_lone(own, at // rounds)
        far, _ = gather_lone(own, at % rounds)
        return at + 1, jnp.maximum(table, score(lone, far))

    table = lax.while_loop(lambda state: state[0] < rounds * rounds, one_round, (jnp.int32(1), table))[1]
    replies = lax.all_to_all(table, AXES, split_axis=0, concat_axis=0, tiled=True)
    return read_reply(replies, cluster, index)


def solution(mesh):
    placed = (P(AXES, None), P(AXES), P(AXES))
    return jax.shard_map(
        shards, mesh=mesh, in_specs=placed, out_specs=P(AXES), check_vma=False
    )
```

profile of v0, /device:TPU:1, one launch (start us, length us, event | category | flops | bytes accessed | tf_op | source)
XLA Modules:
  0.0 97.5 jit_solution(1869934925150235658)
XLA Ops:
  0.0 6.6 %pack.1 = (bf16[64,2,104,128]{3,2,1,0:T(8,128)(2,1)}, s32[2,1024]{1,0:T(2,128)}) custom-call(bf16[1024,768]{1,0:T(8,128)(2,1)} %emb_ref.1, s32[1,1024]{1,0:T(1,128)} %bitcast.16, s32[1,1024]{1,0:T(1,128)} %bitcast.18), custom_call_target="tpu_custom_call" | custom-call | tf_op jit(solution)/shard_map/pack/pallas_call | solution.py:183
  6.6 56.5 %all_to_all.16.msg_ref.own_ref = bf16[128,104,128]{2,1,0:T(8,128)(2,1)S(1)} all-to-all(bf16[128,104,128]{2,1,0:T(8,128)(2,1)} %bitcast.13), channel_id=1, replica_groups=mesh['owner'=32,'split'=4] {'owner','split'}, dimensions={0} | all-to-all | bytes 6815744 | tf_op jit(solution)/shard_map/all_to_all | solution.py:530
  63.1 0.3 collective-permute-start.4
  63.4 2.3 %lone.9 = (bf16[272,768]{1,0:T(8,128)(2,1)}, s32[1,1]{1,0:T(1,128)}) custom-call(bf16[128,104,128]{2,1,0:T(8,128)(2,1)S(1)} %all_to_all.16.msg_ref.own_ref), custom_call_target="tpu_custom_call" | custom-call | tf_op jit(solution)/shard_map/lone/pallas_call | solution.py:291
  65.7 0.3 collective-permute-start.2
  66.0 0.3 collective-permute-start.3
  67.0 3.1 %collective-permute-done.2.beside_ref = bf16[272,768]{1,0:T(8,128)(2,1)} collective-permute-done((bf16[272,768]{1,0:T(8,128)(2,1)}, bf16[272,768]{1,0:T(8,128)(2,1)}, u32[]{:S(2)}, u32[]{:S(2)}) %collective-permute-start.2) | collective-permute-done | bytes 417824 | tf_op jit(solution)/shard_map/ppermute | solution.py:534
  70.1 0.0 collective-permute-done.4.other_ref
  70.1 9.0 %pairs.5 = (f32[2,2048]{1,0:T(2,128)}, f32[1,256]{1,0:T(1,128)}) custom-call(bf16[128,104,128]{2,1,0:T(8,128)(2,1)S(1)} %all_to_all.16.msg_ref.own_ref, bf16[128,104,128]{2,1,0:T(8,128)(2,1)} %collective-permute-done.4.other_ref, bf16[272,768]{1,0:T(8,128)(2,1)} %get-tuple-element.99.lone_ref, bf16[272,768]{1,0:T(8,128)(2,1)} %collective-permute-done.2.beside_ref), custom_call_target="tpu_custom_call" | custom-call | tf_op jit(solution)/shard_map/pairs/pallas_call | solution.py:387
  79.2 0.0 collective-permute-done.3.late_ref
  79.2 2.3 %finish.5 = f32[128,128]{1,0:T(8,128)S(1)} custom-call(bf16[272,768]{1,0:T(8,128)(2,1)} %get-tuple-element.99.lone_ref, bf16[272,768]{1,0:T(8,128)(2,1)} %collective-permute-done.2.beside_ref, bf16[272,768]{1,0:T(8,128)(2,1)} %collective-permute-done.3.late_ref, f32[2,2048]{1,0:T(2,128)} %get-tuple-element.100.best_ref, f32[1,256]{1,0:T(1,128)} %get-tuple-element.101.found_ref), custom_call_target="tpu_custom_call" | custom-call | tf_op jit(solution)/shard_map/finish/pallas_call | solution.py:464
  81.5 14.1 %all_to_all.17 = f32[128,1,128]{2,1,0:T(1,128)} all-to-all(f32[128,1,128]{2,1,0:T(1,128)S(1)} %bitcast.14), channel_id=1, replica_groups=mesh['owner'=32,'split'=4] {'owner','split'}, dimensions={0} | all-to-all | bytes 131072 | tf_op jit(solution)/shard_map/all_to_all | solution.py:550
  95.6 1.9 %reply.1 = f32[1,1024]{1,0:T(1,128)} custom-call(f32[128,128]{1,0:T(8,128)} %bitcast.15, s32[1,1024]{1,0:T(1,128)} %bitcast.17, s32[2,1024]{1,0:T(2,128)} %get-tuple-element.104.index_ref), custom_call_target="tpu_custom_call" | custom-call | tf_op jit(solution)/shard_map/reply/pallas_call | solution.py:499
  (1 shorter events, 0.0 us)
Async XLA Ops:
  63.1 7.0 %collective-permute-start.4 = (bf16[128,104,128]{2,1,0:T(8,128)(2,1)S(1)}, bf16[128,104,128]{2,1,0:T(8,128)(2,1)}, u32[]{:S(2)}, u32[]{:S(2)}) collective-permute-start(bf16[128,104,128]{2,1,0:T(8,128)(2,1)S(1)} %all_to_all.16.msg_ref.own_ref), channel_id=1, source_target_pairs={{0,4},{1,5},{2,6},{3,7},{4,0},{5,1},{6,2},{7,3},{8,12},{9,13},{10,... | collective-permute-start | bytes 10223624 | tf_op jit(solution)/shard_map/ppermute | solution.py:531
  65.7 4.4 %collective-permute-start.2 = (bf16[272,768]{1,0:T(8,128)(2,1)}, bf16[272,768]{1,0:T(8,128)(2,1)}, u32[]{:S(2)}, u32[]{:S(2)}) collective-permute-start(bf16[272,768]{1,0:T(8,128)(2,1)} %get-tuple-element.99.lone_ref), channel_id=1, source_target_pairs={{0,4},{1,5},{2,6},{3,7},{4,0},{5,1},{6,2},{7,3},{8,12},{9,13},{10,... | collective-permute-start | bytes 1253384 | tf_op jit(solution)/shard_map/ppermute | solution.py:534
  66.0 13.2 %collective-permute-start.3 = (bf16[272,768]{1,0:T(8,128)(2,1)}, bf16[272,768]{1,0:T(8,128)(2,1)}, u32[]{:S(2)}, u32[]{:S(2)}) collective-permute-start(bf16[272,768]{1,0:T(8,128)(2,1)} %get-tuple-element.99.lone_ref), channel_id=1, source_target_pairs={{0,1},{1,0},{2,3},{3,2},{4,5},{5,4},{6,7},{7,6},{8,9},{9,8},{10,11... | collective-permute-start | bytes 1253384 | tf_op jit(solution)/shard_map/ppermute | solution.py:535
where the time goes:
time: 97.8 us; the launch traced here: 97.5 us
  blocking collectives  70.7 us (72%)
  Pallas kernels  22.2 us (23%)
  waiting for transfers between devices  3.15 us (3%)
    all_to_all x1, blocking collectives, shards(): own = lax.all_to_all(message, AXES, split_axis=0, concat_axis=0, tiled=True)  56.5 us
    all_to_all x1, blocking collectives, shards(): lax.all_to_all(table, AXES, split_axis=0, concat_axis=0, tiled=True)  14.1 us
    pallas_call x1, Pallas kernels, score_pairs(): pl.pallas_call(pairs_kernel, in_specs=[pl.BlockSpec(memory_space=pltpu.VM...  9.03 us
    pallas_call x1, Pallas kernels, pack(): pl.pallas_call(pack_kernel, grid=(steps,), in_specs=[pl.BlockSpec((rows,...  6.62 us
    ppermute x1, waiting for transfers between devices, score(): beside = lax.ppermute(lone, AXES, SWAP)  3.14 us
    pallas_call x1, Pallas kernels, gather_lone(): pl.pallas_call(lone_kernel if some else functools.partial(lone_kernel, No...  2.34 us
    pallas_call x1, Pallas kernels, finish(): pl.pallas_call(finish_kernel, in_specs=[pl.BlockSpec(memory_space=pltpu.V...  2.28 us
  transfers between devices with their start and end apart: 3, of which 1 were waited for; matrix products, arithmetic and copies ran while one was open for 0% of the time, Pallas kernels for 12%

commit v1 on v0

--- a/solution.py
+++ b/solution.py
@@ -9,6 +9,7 @@
 
 D = 768
 LANES = 128
+HALF = LANES // 2
 BLOCKS = D // LANES
 SLOTS = 16
 DATA = SLOTS * BLOCKS
@@ -23,7 +24,7 @@
 FAR = float(2**20)
 BLOCK = 512
 AXES = ("owner", "split")
-VMEM = 56 * 2**20
+MIB = 2**20
 
 
 def slot_of(index):
@@ -205,7 +206,7 @@
             pltpu.VMEM((4, PEERS, LANES), jnp.float32),
             pltpu.SMEM((1,), jnp.int32),
         ],
-        compiler_params=pltpu.CompilerParams(vmem_limit_bytes=VMEM),
+        compiler_params=pltpu.CompilerParams(vmem_limit_bytes=24 * MIB),
         name="pack",
     )(embeddings, cluster.reshape(1, rows), order.reshape(1, rows))
     return message.reshape(PEERS, MSG, LANES), index
@@ -297,7 +298,7 @@
             jax.ShapeDtypeStruct((LONE + FACTS, D), jnp.bfloat16),
             jax.ShapeDtypeStruct((1, 1), jnp.int32),
         ],
-        compiler_params=pltpu.CompilerParams(vmem_limit_bytes=VMEM),
+        compiler_params=pltpu.CompilerParams(vmem_limit_bytes=16 * MIB),
         name="lone",
     )(*some, msg)
 
@@ -327,56 +328,65 @@
     return rank_from(facts[0:1, :], facts[1:2, :]), peer, facts[3:4, :].astype(jnp.int32)
 
 
-def pairs_kernel(own_ref, other_ref, lone_ref, beside_ref, out_ref, found_ref, rank_ref, rows_ref, cols_ref, some_ref):
+def pairs_kernel(
+    own_ref, other_ref, lone_ref, beside_ref, out_ref, found_ref, rank_ref, rows_ref, cols_ref, some_ref
+):
     core, late = my_core(), my_late()
+
+    @pl.when(late == 1)
+    def _():
+        some_ref[...] = lone_ref[...]
+
+    @pl.when(late == 0)
+    def _():
+        some_ref[...] = beside_ref[...]
+
     own_ranks = ranks_of(own_ref)
     as_columns(own_ranks, rank_ref)
     count = ROWS // BLOCK
-    rows_ref[...] = jnp.full((ROWS, LANES), -1.0, jnp.float32)
     cols_ref[...] = jnp.full((8, ROWS), -1.0, jnp.float32)
-
-    def score(right_ref, row, i, j, both):
-        scores = dot_nt(units_of(own_ref, i * BLOCK, BLOCK), units_of(right_ref, j * BLOCK, BLOCK))
-        earlier = row[:, span(j)] < wide(rank_ref[span(i), :], BLOCK)
-        kept = narrow_rows(jnp.where(earlier, scores, -1.0))
-        rows_ref[span(i), :] = jnp.maximum(rows_ref[span(i), :], kept)
-        if both:
-            kept = narrow_cols(jnp.where(earlier, -1.0, scores))
-            cols_ref[:, span(j)] = jnp.maximum(cols_ref[:, span(j)], kept)
-
-    @pl.when(late == 0)
-    def _():
-        row = as_row(own_ranks)
-        for i in range(count):
-            for j in range(i, count):
-                score(own_ref, row, i, j, i != j)
-        some_ref[...] = beside_ref[...]
-
-    def across(firsts, seconds):
-        row = as_row(ranks_of(other_ref))
-        for i in firsts:
-            for j in seconds:
-                score(other_ref, row, i, j, True)
-        some_ref[...] = lone_ref[...]
-
-    @pl.when((late == 1) & (core == 0))
-    def _():
-        across(range(count), range(count // 2))
-
-    @pl.when((late == 1) & (core == 1))
-    def _():
-        across(range(count // 2, count), range(count))
-
     some = some_ref[:LONE, :]
     some_rank, _, _ = lone_facts(some_ref)
     found = jnp.full((8, LONE), -1.0, jnp.float32)
     for i in range(count):
         scores = dot_nt(units_of(own_ref, i * BLOCK, BLOCK), some)
         rank = wide(rank_ref[span(i), :], LONE)
-        kept = narrow_rows(jnp.where(some_rank < rank, scores, -1.0))
-        rows_ref[span(i), :] = jnp.maximum(rows_ref[span(i), :], kept)
+        rows_ref[span(i), :] = narrow_rows(jnp.where(some_rank < rank, scores, -1.0))
         found = jnp.maximum(found, narrow_cols(jnp.where(rank < some_rank, scores, -1.0)))
     found_ref[...] = jnp.max(found, axis=0, keepdims=True)
+
+    def score(right_ref, row, i, j, size, both):
+        left_at, right_at = slice(i * size, (i + 1) * size), slice(j * size, (j + 1) * size)
+        scores = dot_nt(units_of(own_ref, i * size, size), units_of(right_ref, j * size, size))
+        earlier = row[:, right_at] < wide(rank_ref[left_at, :], size)
+        kept = narrow_rows(jnp.where(earlier, scores, -1.0))
+        rows_ref[left_at, :] = jnp.maximum(rows_ref[left_at, :], kept)
+        if both:
+            kept = narrow_cols(jnp.where(earlier, -1.0, scores))
+            cols_ref[:, right_at] = jnp.maximum(cols_ref[:, right_at], kept)
+
+    @pl.when(late == 0)
+    def _():
+        row = as_row(own_ranks)
+        size = BLOCK // 2
+        for i in range(2 * count):
+            for j in range(i, 2 * count):
+                score(own_ref, row, i, j, size, i != j)
+
+    def across(firsts, seconds):
+        row = as_row(ranks_of(other_ref))
+        for i in firsts:
+            for j in seconds:
+                score(other_ref, row, i, j, BLOCK, True)
+
+    @pl.when((late == 1) & (core == 0))
+    def _():
+        across(range(count), range(count // 2))
+
+    @pl.when((late == 1) & (core == 1))
+    def _():
+        across(range(count // 2, count), range(count))
+
     own_best = row_of_best(rows_ref)
     cols_best = jnp.max(cols_ref[...], axis=0, keepdims=True)
     out_ref[0:1, :] = jnp.where(late == 0, jnp.maximum(own_best, cols_best), own_best)
@@ -384,10 +394,11 @@
 
 
 def score_pairs(own, other, lone, beside):
+    vmem = pl.BlockSpec(memory_space=pltpu.VMEM)
     return pl.pallas_call(
         pairs_kernel,
-        in_specs=[pl.BlockSpec(memory_space=pltpu.VMEM)] * 4,
-        out_specs=[pl.BlockSpec(memory_space=pltpu.VMEM)] * 2,
+        in_specs=[vmem] * 4,
+        out_specs=[vmem] * 2,
         out_shape=[
             jax.ShapeDtypeStruct((2, ROWS), jnp.float32),
             jax.ShapeDtypeStruct((1, LONE), jnp.float32),
@@ -398,7 +409,7 @@
             pltpu.VMEM((8, ROWS), jnp.float32),
             pltpu.VMEM((LONE + FACTS, D), jnp.bfloat16),
         ],
-        compiler_params=pltpu.CompilerParams(vmem_limit_bytes=VMEM),
+        compiler_params=pltpu.CompilerParams(vmem_limit_bytes=20 * MIB),
         name="pairs",
     )(own, other, lone, beside)
 
@@ -446,18 +457,20 @@
         [found[0][2] + SLOTS * core, found[1][2] + SLOTS * (1 - core), late_slot + 2 * SLOTS], axis=1
     )
     at_peer = ones_where(iota((PEERS, 3 * LONE), 0) == peer)
-    at_slot = iota((LANES, 3 * LONE), 0) == slot
-    placed = dot_nt(at_peer, ones_where(at_slot))
-    value = jnp.where(at_slot, best, 0.0)
-    value = sum(dot_nt(at_peer, part) for part in thirds(value))
-    table = jnp.where(placed > 0.5, value, -1.0)
+    at_slot = iota((HALF, 3 * LONE), 0) == slot
+    first, second, third = (part.astype(jnp.float32) for part in thirds(best))
+    sums = jnp.concatenate([jnp.where(at_slot, part, 0.0) for part in (first, 1.0, second, third)], axis=0)
+    sums = dot_nt(at_peer, sums.astype(jnp.bfloat16))
+    front, back = sums[:, :LANES], sums[:, LANES:]
+    value = front + (back + pltpu.roll(back, HALF, 1))
+    table = jnp.where(pltpu.roll(front, HALF, 1) > 0.5, value, -1.0)
     lane = iota((PEERS, LANES), 1)
     rest = jnp.where(
         lane >> 4 == core,
         as_table(best_ref[0:1, :]),
         jnp.where(lane < 2 * SLOTS, as_table(best_ref[1:2, :]), -1.0),
     )
-    out_ref[...] = jnp.maximum(table, rest)
+    out_ref[...] = jnp.where(lane < HALF, jnp.maximum(table, rest), -1.0)
 
 
 def finish(lone, beside, late_rows, best, found):
@@ -466,7 +479,7 @@
         in_specs=[pl.BlockSpec(memory_space=pltpu.VMEM)] * 5,
         out_specs=pl.BlockSpec(memory_space=pltpu.VMEM),
         out_shape=jax.ShapeDtypeStruct((PEERS, LANES), jnp.float32),
-        compiler_params=pltpu.CompilerParams(vmem_limit_bytes=VMEM),
+        compiler_params=pltpu.CompilerParams(vmem_limit_bytes=8 * MIB),
         name="finish",
     )(lone, beside, late_rows, best, found)
 
@@ -487,7 +500,9 @@
     late = jnp.maximum(pltpu.roll(early, PEERS - 1, 0), beside)
     both = jnp.concatenate([early.T[:2 * SLOTS, :], late.T[:2 * SLOTS, :]], axis=0)
     chosen = ones_where(iota((PEERS, rows), 0) == pair_of(cluster, jnp.zeros_like(index)) * 2)
-    picked = sum(dot_nn(part, chosen) for part in thirds(both))
+    picked = dot_nn(jnp.concatenate(thirds(both), axis=0), chosen)
+    size = 4 * SLOTS
+    picked = picked[:size, :] + (picked[size:2 * size, :] + picked[2 * size:, :])
     at = (index & 1) * SLOTS + slot_of(index)
     here = iota((4 * SLOTS, rows), 0)
     here = ((here == at) & (index < 32)) | ((here == at + 2 * SLOTS) & (index + 32 >= count))
@@ -501,7 +516,7 @@
         in_specs=[pl.BlockSpec(memory_space=pltpu.VMEM)] * 3,
         out_specs=pl.BlockSpec(memory_space=pltpu.VMEM),
         out_shape=jax.ShapeDtypeStruct((1, rows), jnp.float32),
-        compiler_params=pltpu.CompilerParams(vmem_limit_bytes=VMEM),
+        compiler_params=pltpu.CompilerParams(vmem_limit_bytes=8 * MIB),
         name="reply",
     )(table, cluster.reshape(1, rows), index)
     return best.reshape(rows)

time: 97.8 us -> 95 us (0.971)
  Pallas kernels: 22.2 us -> 18.7 us
  local copies, waits for them, and re-layouts: 0 us -> 2.79 us
  waiting for transfers between devices: 3.15 us -> 1.34 us
    unnamed x0 -> x8, local copies, waits for them, and re-layouts: none -> 2.79 us
    pallas_call x1, Pallas kernels: 6.62 us -> 4.01 us  [pack(): pl.pallas_call(pack_kernel, grid=(steps,), in_specs=[pl.BlockSpec((rows,...]
    ppermute x1, waiting for transfers between devices: 3.14 us -> 1.06 us  [score(): beside = lax.ppermute(lone, AXES, SWAP)]
    pallas_call x1, Pallas kernels: 2.34 us -> 4.09 us  [gather_lone(): pl.pallas_call(lone_kernel if some else functools.partial(lone_kernel, No...]
    pallas_call x1, Pallas kernels: 2.28 us -> 0.86 us  [finish(): pl.pallas_call(finish_kernel, in_specs=[pl.BlockSpec(memory_space=pltpu.V...]
  transfers between devices with their start and end apart: 3 -> 3, of which waited for: 1 -> 2; matrix products, arithmetic and copies ran while one was open for 0% -> 0% of each run, Pallas kernels for 12% -> 13%
where the time goes in v1:
time: 95 us; the launch traced here: 94.7 us
  blocking collectives  70.3 us (74%)
  Pallas kernels  18.7 us (20%)
  local copies, waits for them, and re-layouts  2.79 us (3%)
  waiting for transfers between devices  1.34 us (1%)
    all_to_all x1, blocking collectives, shards(): own = lax.all_to_all(message, AXES, split_axis=0, concat_axis=0, tiled=True)  56.4 us
    all_to_all x1, blocking collectives, shards(): lax.all_to_all(table, AXES, split_axis=0, concat_axis=0, tiled=True)  13.9 us
    pallas_call x1, Pallas kernels, score_pairs(): pl.pallas_call(pairs_kernel, in_specs=[vmem] * 4, out_specs=[vmem] * 2, o...  8.67 us
    pallas_call x1, Pallas kernels, gather_lone(): pl.pallas_call(lone_kernel if some else functools.partial(lone_kernel, No...  4.09 us
    pallas_call x1, Pallas kernels, pack(): pl.pallas_call(pack_kernel, grid=(steps,), in_specs=[pl.BlockSpec((rows,...  4.01 us
    unnamed x8, local copies, waits for them, and re-layouts  2.79 us
  transfers between devices with their start and end apart: 3, of which 2 were waited for; matrix products, arithmetic and copies ran while one was open for 0% of the time, Pallas kernels for 13%

profile of v1, /device:TPU:1, one launch (start us, length us, event | category | flops | bytes accessed | tf_op | source)
XLA Modules:
  0.0 94.7 jit_solution(15728927053432295036)
XLA Ops:
  0.0 0.0 copy-start
  0.0 1.4 %copy-done = bf16[1024,768]{1,0:T(8,128)(2,1)S(1)} copy-done((bf16[1024,768]{1,0:T(8,128)(2,1)S(1)}, bf16[1024,768]{1,0:T(8,128)(2,1)}, u32[]{:S(2)}) %copy-start) | copy-done | bytes 1572888
  1.4 0.0 copy-start.1
  1.4 0.7 copy-done.1
  2.1 0.0 copy-start.3
  2.1 0.7 copy-done.3
  2.8 4.0 %pack.1 = (bf16[64,2,104,128]{3,2,1,0:T(8,128)(2,1)S(1)}, s32[2,1024]{1,0:T(2,128)S(1)}) custom-call(bf16[1024,768]{1,0:T(8,128)(2,1)S(1)} %copy-done, s32[1,1024]{1,0:T(1,128)S(1)} %bitcast.15, s32[1,1024]{1,0:T(1,128)S(1)} %bitcast.17), custom_call_target="tpu_custom_call" | custom-call | tf_op jit(solution)/shard_map/pack/pallas_call | solution.py:184
  6.8 56.4 %all_to_all.16.msg_ref.own_ref = bf16[128,104,128]{2,1,0:T(8,128)(2,1)} all-to-all(bf16[128,104,128]{2,1,0:T(8,128)(2,1)S(1)} %bitcast.13), channel_id=1, replica_groups=mesh['owner'=32,'split'=4] {'owner','split'}, dimensions={0} | all-to-all | bytes 6815744 | tf_op jit(solution)/shard_map/all_to_all | solution.py:545
  63.3 0.3 collective-permute-start.4
  63.5 4.1 %lone.9 = (bf16[272,768]{1,0:T(8,128)(2,1)S(1)}, s32[1,1]{1,0:T(1,128)}) custom-call(bf16[128,104,128]{2,1,0:T(8,128)(2,1)} %all_to_all.16.msg_ref.own_ref), custom_call_target="tpu_custom_call" | custom-call | tf_op jit(solution)/shard_map/lone/pallas_call | solution.py:292
  67.6 0.3 collective-permute-start.2
  67.9 0.3 collective-permute-start.3
  68.8 1.1 %collective-permute-done.2.beside_ref = bf16[272,768]{1,0:T(8,128)(2,1)S(1)} collective-permute-done((bf16[272,768]{1,0:T(8,128)(2,1)S(1)}, bf16[272,768]{1,0:T(8,128)(2,1)S(1)}, u32[]{:S(2)}, u32[]{:S(2)}) %collective-permute-start.2) | collective-permute-done | bytes 417824 | tf_op jit(solution)/shard_map/ppermute | solution.py:549
  69.9 0.0 collective-permute-done.4.other_ref
  69.9 8.7 %pairs.5 = (f32[2,2048]{1,0:T(2,128)S(1)}, f32[1,256]{1,0:T(1,128)S(1)}) custom-call(bf16[128,104,128]{2,1,0:T(8,128)(2,1)} %all_to_all.16.msg_ref.own_ref, bf16[128,104,128]{2,1,0:T(8,128)(2,1)} %collective-permute-done.4.other_ref, bf16[272,768]{1,0:T(8,128)(2,1)S(1)} %get-tuple-element.99.lone_ref, bf16[272,768]{1,0:T(8,128)(2,1)S(1)} %collective-permute-done.2.beside_ref), custom_call_target="tpu_custom_call" | custom-call | tf_op jit(solution)/shard_map/pairs/pallas_call | solution.py:398
  78.6 0.3 collective-permute-done.3.late_ref
  78.8 0.9 finish.5
  79.7 0.0 copy-start.2
  79.7 13.9 %all_to_all.17 = f32[128,1,128]{2,1,0:T(1,128)S(1)} all-to-all(f32[128,1,128]{2,1,0:T(1,128)S(1)} %bitcast.18), channel_id=1, replica_groups=mesh['owner'=32,'split'=4] {'owner','split'}, dimensions={0} | all-to-all | bytes 131072 | tf_op jit(solution)/shard_map/all_to_all | solution.py:565
  93.6 0.0 copy-done.2
  93.6 1.1 %reply.1 = f32[1,1024]{1,0:T(1,128)} custom-call(f32[128,128]{1,0:T(8,128)S(1)} %bitcast.14, s32[1,1024]{1,0:T(1,128)S(1)} %bitcast.16, s32[2,1024]{1,0:T(2,128)S(1)} %get-tuple-element.104.index_ref), custom_call_target="tpu_custom_call" | custom-call | tf_op jit(solution)/shard_map/reply/pallas_call | solution.py:514
  (1 shorter events, 0.0 us)
Async XLA Ops:
  0.0 1.4 %copy-start = (bf16[1024,768]{1,0:T(8,128)(2,1)S(1)}, bf16[1024,768]{1,0:T(8,128)(2,1)}, u32[]{:S(2)}) copy-start(bf16[1024,768]{1,0:T(8,128)(2,1)} %emb_ref.1) | copy-start | bytes 4718596
  1.4 0.7 copy-start.1
  2.1 0.7 copy-start.3
  63.3 6.6 %collective-permute-start.4 = (bf16[128,104,128]{2,1,0:T(8,128)(2,1)}, bf16[128,104,128]{2,1,0:T(8,128)(2,1)}, u32[]{:S(2)}, u32[]{:S(2)}) collective-permute-start(bf16[128,104,128]{2,1,0:T(8,128)(2,1)} %all_to_all.16.msg_ref.own_ref), channel_id=1, source_target_pairs={{0,4},{1,5},{2,6},{3,7},{4,0},{5,1},{6,2},{7,3},{8,12},{9,13},{10,... | collective-permute-start | bytes 10223624 | tf_op jit(solution)/shard_map/ppermute | solution.py:546
  67.6 2.3 %collective-permute-start.2 = (bf16[272,768]{1,0:T(8,128)(2,1)S(1)}, bf16[272,768]{1,0:T(8,128)(2,1)S(1)}, u32[]{:S(2)}, u32[]{:S(2)}) collective-permute-start(bf16[272,768]{1,0:T(8,128)(2,1)S(1)} %get-tuple-element.99.lone_ref), channel_id=1, source_target_pairs={{0,4},{1,5},{2,6},{3,7},{4,0},{5,1},{6,2},{7,3},{8,12},{9,13},{10,... | collective-permute-start | bytes 1253384 | tf_op jit(solution)/shard_map/ppermute | solution.py:549
  67.9 11.0 %collective-permute-start.3 = (bf16[272,768]{1,0:T(8,128)(2,1)S(1)}, bf16[272,768]{1,0:T(8,128)(2,1)S(1)}, u32[]{:S(2)}, u32[]{:S(2)}) collective-permute-start(bf16[272,768]{1,0:T(8,128)(2,1)S(1)} %get-tuple-element.99.lone_ref), channel_id=1, source_target_pairs={{0,1},{1,0},{2,3},{3,2},{4,5},{5,4},{6,7},{7,6},{8,9},{9,8},{10,11... | collective-permute-start | bytes 1253384 | tf_op jit(solution)/shard_map/ppermute | solution.py:550
  79.7 13.9 %copy-start.2 = (s32[1024]{0:T(1024)S(1)}, s32[1024]{0:T(1024)}, u32[]{:S(2)}) copy-start(s32[1024]{0:T(1024)} %param.6) | copy-start | bytes 12292

commit v2 on v1

--- a/solution.py
+++ b/solution.py
@@ -66,7 +66,10 @@
     return first, second, (left - second.astype(jnp.float32)).astype(jnp.bfloat16)
 
 
-def pack_kernel(emb_ref, cluster_ref, order_ref, out_ref, index_ref, unit_ref, at_ref, some_ref, some_at_ref, late_ref, meta_ref, past_ref):
+def pack_kernel(
+    emb_hbm, cluster_hbm, order_hbm, out_ref, index_ref, emb_ref, cluster_ref, order_ref, sems, unit_ref, at_ref,
+    some_ref, some_at_ref, late_ref, meta_ref, past_ref
+):
     step = pl.program_id(0)
     rows = emb_ref.shape[0]
     pairs = PEERS // 2
@@ -74,9 +77,19 @@
 
     @pl.when(step == 0)
     def _():
-        values = emb_ref[...].astype(jnp.float32)
-        total = jnp.sum(values * values, axis=1, keepdims=True)
-        unit_ref[...] = (values * lax.rsqrt(total + 1e-06)).astype(jnp.bfloat16)
+        chunk = rows // 4
+        spans = [slice(i * chunk, (i + 1) * chunk) for i in range(4)]
+        fetches = [
+            pltpu.make_async_copy(cluster_hbm, cluster_ref, sems.at[4]),
+            pltpu.make_async_copy(order_hbm, order_ref, sems.at[5]),
+        ] + [
+            pltpu.make_async_copy(emb_hbm.at[at, :], emb_ref.at[at, :], sems.at[i])
+            for i, at in enumerate(spans)
+        ]
+        for fetch in fetches:
+            fetch.start()
+        fetches[0].wait()
+        fetches[1].wait()
         cluster = cluster_ref[...]
         rank = order_ref[...]
         hit = iota((CLUSTERS, rows), 0) == cluster
@@ -126,6 +139,11 @@
         place = iota((PEERS, CLUSTERS), 0) & (pairs - 1)
         theirs = ones_where((place >> 2) * 2 + (place & 1) == iota((PEERS, CLUSTERS), 1))
         meta_ref[3] = dot_nn(theirs, counts.astype(jnp.bfloat16))
+        for fetch, at in zip(fetches[2:], spans):
+            fetch.wait()
+            values = emb_ref[at, :].astype(jnp.float32)
+            total = jnp.sum(values * values, axis=1, keepdims=True)
+            unit_ref[at, :] = (values * lax.rsqrt(total + 1e-06)).astype(jnp.bfloat16)
 
     def bring(chunk):
         start = chunk * LANES
@@ -184,11 +202,7 @@
     message, index = pl.pallas_call(
         pack_kernel,
         grid=(steps,),
-        in_specs=[
-            pl.BlockSpec((rows, D), lambda i: (0, 0)),
-            pl.BlockSpec((1, rows), lambda i: (0, 0)),
-            pl.BlockSpec((1, rows), lambda i: (0, 0)),
-        ],
+        in_specs=[pl.BlockSpec(memory_space=pltpu.HBM)] * 3,
         out_specs=[
             pl.BlockSpec((PEERS // 2 // steps, 2, MSG, LANES), lambda i: (i, 0, 0, 0)),
             pl.BlockSpec((2, rows), lambda i: (0, 0)),
@@ -198,6 +212,10 @@
             jax.ShapeDtypeStruct((2, rows), jnp.int32),
         ],
         scratch_shapes=[
+            pltpu.VMEM((rows, D), jnp.bfloat16),
+            pltpu.VMEM((1, rows), jnp.int32),
+            pltpu.VMEM((1, rows), jnp.int32),
+            pltpu.SemaphoreType.DMA((6,)),
             pltpu.VMEM((rows, D), jnp.bfloat16),
             pltpu.VMEM((8, rows), jnp.int32),
             pltpu.VMEM((rows // 2, D), jnp.bfloat16),
@@ -206,7 +224,7 @@
             pltpu.VMEM((4, PEERS, LANES), jnp.float32),
             pltpu.SMEM((1,), jnp.int32),
         ],
-        compiler_params=pltpu.CompilerParams(vmem_limit_bytes=24 * MIB),
+        compiler_params=pltpu.CompilerParams(vmem_limit_bytes=121 * MIB // 2),
         name="pack",
     )(embeddings, cluster.reshape(1, rows), order.reshape(1, rows))
     return message.reshape(PEERS, MSG, LANES), index
@@ -257,14 +275,17 @@
     )
 
 
-def lone_kernel(round_ref, msg_ref, out_ref, most_ref):
+def lone_kernel(round_ref, msg_ref, out_ref, rounds_ref, more_ref):
     core = my_core()
     first = 0 if round_ref is None else round_ref[0] * LONE
     held, meta = meta_of(msg_ref)
     high, low, count = (held[:, i:i + 1, :] for i in (0, 1, 3))
     half = jnp.floor((jnp.maximum(meta[:, :, 2, :] - 32.0, 0.0) + 1.0) * 0.5)
     most = jnp.sum(jnp.sum(half, axis=0), axis=0, keepdims=True)
-    most_ref[...] = jnp.max(most, axis=1, keepdims=True).astype(jnp.int32)
+    most = jnp.max(most, axis=1, keepdims=True).astype(jnp.int32)
+    rounds = (most + LONE - 1) // LONE
+    rounds_ref[...] = rounds
+    more_ref[...] = rounds * rounds - 1
 
     index = (2 * (iota((GROUPS, 1, LANES), 2) & 15) + core + 32).astype(jnp.float32)
     lone = jnp.where(index < count, 1.0, 0.0)
@@ -293,9 +314,10 @@
         lone_kernel if some else functools.partial(lone_kernel, None),
         in_specs=[pl.BlockSpec(memory_space=pltpu.SMEM)] * len(some)
         + [pl.BlockSpec(memory_space=pltpu.VMEM)],
-        out_specs=[pl.BlockSpec(memory_space=pltpu.VMEM)] * 2,
+        out_specs=[pl.BlockSpec(memory_space=pltpu.VMEM)] * 3,
         out_shape=[
             jax.ShapeDtypeStruct((LONE + FACTS, D), jnp.bfloat16),
+            jax.ShapeDtypeStruct((1, 1), jnp.int32),
             jax.ShapeDtypeStruct((1, 1), jnp.int32),
         ],
         compiler_params=pltpu.CompilerParams(vmem_limit_bytes=16 * MIB),
@@ -543,25 +565,25 @@
 def shards(embeddings, cluster, order):
     message, index = pack(embeddings, cluster, order)
     own = lax.all_to_all(message, AXES, split_axis=0, concat_axis=0, tiled=True)
-    other = lax.ppermute(own, AXES, SWAP)
-
-    def score(lone, far):
+
+    def score(other, lone, far):
         beside = lax.ppermute(lone, AXES, SWAP)
         far = lax.ppermute(far, AXES, OTHER_CHIP)
         best, found = score_pairs(own, other, lone, beside)
         return finish(lone, beside, far, best, found)
 
-    lone, most = gather_lone(own)
-    table = score(lone, lone)
-    rounds = (most[0, 0] + LONE - 1) // LONE
+    other = lax.ppermute(own, AXES, SWAP)
+    lone, rounds, more = gather_lone(own)
+    table = score(other, lone, lone)
 
     def one_round(state):
-        at, table = state
-        lone, _ = gather_lone(own, at // rounds)
-        far, _ = gather_lone(own, at % rounds)
-        return at + 1, jnp.maximum(table, score(lone, far))
-
-    table = lax.while_loop(lambda state: state[0] < rounds * rounds, one_round, (jnp.int32(1), table))[1]
+        left, table = state
+        other = lax.ppermute(own, AXES, SWAP)
+        lone = gather_lone(own, lax.div(left, rounds[0, 0]))[0]
+        far = gather_lone(own, lax.rem(left, rounds[0, 0]))[0]
+        return left - 1, jnp.maximum(table, score(other, lone, far))
+
+    table = lax.while_loop(lambda state: state[0] > 0, one_round, (more[0, 0], table))[1]
     replies = lax.all_to_all(table, AXES, split_axis=0, concat_axis=0, tiled=True)
     return read_reply(replies, cluster, index)
 

time: 95 us -> 93.1 us (0.980)
  waiting for transfers between devices: 1.34 us -> 4.8 us
  local copies, waits for them, and re-layouts: 2.79 us -> 0.02 us
  Pallas kernels: 18.7 us -> 16.1 us
    pallas_call x1, Pallas kernels: 8.67 us -> 5.86 us  [score_pairs(): pl.pallas_call(pairs_kernel, in_specs=[vmem] * 4, out_specs=[vmem] * 2, o...]
    unnamed x8, local copies, waits for them, and re-layouts: 2.79 us -> 0.02 us
    ppermute x1, waiting for transfers between devices: 1.06 us -> 3.68 us  [score(): beside = lax.ppermute(lone, AXES, SWAP)]
    pallas_call x1, Pallas kernels: 4.01 us -> 6.17 us  [pack(): pl.pallas_call(pack_kernel, grid=(steps,), in_specs=[pl.BlockSpec(memory_...]
    pallas_call x1, Pallas kernels: 4.09 us -> 2.14 us  [gather_lone(): pl.pallas_call(lone_kernel if some else functools.partial(lone_kernel, No...]
  transfers between devices with their start and end apart: 3 -> 3, of which waited for: 2 -> 2; matrix products, arithmetic and copies ran while one was open for 0% -> 0% of each run, Pallas kernels for 13% -> 9%
where the time goes in v2:
time: 93.1 us; the launch traced here: 92.8 us
  blocking collectives  70.4 us (76%)
  Pallas kernels  16.1 us (17%)
  waiting for transfers between devices  4.8 us (5%)
    all_to_all x1, blocking collectives, shards(): own = lax.all_to_all(message, AXES, split_axis=0, concat_axis=0, tiled=True)  56.6 us
    all_to_all x1, blocking collectives, shards(): lax.all_to_all(table, AXES, split_axis=0, concat_axis=0, tiled=True)  13.9 us
    pallas_call x1, Pallas kernels, pack(): pl.pallas_call(pack_kernel, grid=(steps,), in_specs=[pl.BlockSpec(memory_...  6.17 us
    pallas_call x1, Pallas kernels, score_pairs(): pl.pallas_call(pairs_kernel, in_specs=[vmem] * 4, out_specs=[vmem] * 2, o...  5.86 us
    ppermute x1, waiting for transfers between devices, score(): beside = lax.ppermute(lone, AXES, SWAP)  3.68 us
    pallas_call x1, Pallas kernels, gather_lone(): pl.pallas_call(lone_kernel if some else functools.partial(lone_kernel, No...  2.14 us
  transfers between devices with their start and end apart: 3, of which 2 were waited for; matrix products, arithmetic and copies ran while one was open for 0% of the time, Pallas kernels for 9%

profile of v2, /device:TPU:1, one launch (start us, length us, event | category | flops | bytes accessed | tf_op | source)
XLA Modules:
  0.0 92.8 jit_solution(16642685035904185223)
XLA Ops:
  0.0 6.2 %pack.1 = (bf16[64,2,104,128]{3,2,1,0:T(8,128)(2,1)}, s32[2,1024]{1,0:T(2,128)}) custom-call(bf16[1024,768]{1,0:T(8,128)(2,1)} %emb_hbm.1, s32[1,1024]{1,0:T(1,128)} %bitcast.17, s32[1,1024]{1,0:T(1,128)} %bitcast.21), custom_call_target="tpu_custom_call" | custom-call | tf_op jit(solution)/shard_map/pack/pallas_call | solution.py:202
  6.2 56.6 %all_to_all.16.msg_ref.own_ref = bf16[128,104,128]{2,1,0:T(8,128)(2,1)S(1)} all-to-all(bf16[128,104,128]{2,1,0:T(8,128)(2,1)} %bitcast.19), channel_id=1, replica_groups=mesh['owner'=32,'split'=4] {'owner','split'}, dimensions={0} | all-to-all | bytes 6815744 | tf_op jit(solution)/shard_map/all_to_all | solution.py:567
  62.7 0.0 copy-start.2
  62.7 0.3 collective-permute-start.4
  63.0 2.1 %lone.9 = (bf16[272,768]{1,0:T(8,128)(2,1)S(1)}, s32[1,1]{1,0:T(1,128)}, s32[1,1]{1,0:T(1,128)}) custom-call(bf16[128,104,128]{2,1,0:T(8,128)(2,1)S(1)} %all_to_all.16.msg_ref.own_ref), custom_call_target="tpu_custom_call" | custom-call | tf_op jit(solution)/shard_map/lone/pallas_call | solution.py:313
  65.1 0.3 collective-permute-start.2
  65.4 0.3 collective-permute-start.3
  65.7 3.7 %collective-permute-done.2.beside_ref = bf16[272,768]{1,0:T(8,128)(2,1)S(1)} collective-permute-done((bf16[272,768]{1,0:T(8,128)(2,1)S(1)}, bf16[272,768]{1,0:T(8,128)(2,1)S(1)}, u32[]{:S(2)}, u32[]{:S(2)}) %collective-permute-start.2) | collective-permute-done | bytes 417824 | tf_op jit(solution)/shard_map/ppermute | solution.py:570
  69.4 0.0 collective-permute-done.4.other_ref
  69.4 0.0 copy-start.3
  69.4 5.9 %pairs.5 = (f32[2,2048]{1,0:T(2,128)S(1)}, f32[1,256]{1,0:T(1,128)S(1)}) custom-call(bf16[128,104,128]{2,1,0:T(8,128)(2,1)S(1)} %all_to_all.16.msg_ref.own_ref, bf16[128,104,128]{2,1,0:T(8,128)(2,1)S(1)} %collective-permute-done.4.other_ref, bf16[272,768]{1,0:T(8,128)(2,1)S(1)} %get-tuple-element.75.lone_ref, ...), custom_call_target="tpu_custom_call" | custom-call | tf_op jit(solution)/shard_map/pairs/pallas_call | solution.py:420
  75.2 0.0 copy-done.2
  75.2 0.0 copy-done.3
  75.3 1.1 %collective-permute-done.3.late_ref = bf16[272,768]{1,0:T(8,128)(2,1)S(1)} collective-permute-done((bf16[272,768]{1,0:T(8,128)(2,1)S(1)}, bf16[272,768]{1,0:T(8,128)(2,1)S(1)}, u32[]{:S(2)}, u32[]{:S(2)}) %collective-permute-start.3) | collective-permute-done | bytes 417824 | tf_op jit(solution)/shard_map/ppermute | solution.py:571
  76.4 0.9 finish.5
  77.2 0.0 copy-start
  77.2 0.0 copy-start.1
  77.3 0.7 while.12
  77.9 13.9 %all_to_all.17 = f32[128,1,128]{2,1,0:T(1,128)S(1)} all-to-all(f32[128,1,128]{2,1,0:T(1,128)S(1)} %bitcast.20), channel_id=1, replica_groups=mesh['owner'=32,'split'=4] {'owner','split'}, dimensions={0} | all-to-all | bytes 131072 | tf_op jit(solution)/shard_map/all_to_all | solution.py:587
  91.8 0.0 copy-done
  91.8 0.0 copy-done.1
  91.8 1.0 %reply.1 = f32[1,1024]{1,0:T(1,128)} custom-call(f32[128,128]{1,0:T(8,128)S(1)} %bitcast.16, s32[1,1024]{1,0:T(1,128)S(1)} %bitcast.18, s32[2,1024]{1,0:T(2,128)S(1)} %copy-done.1), custom_call_target="tpu_custom_call" | custom-call | tf_op jit(solution)/shard_map/reply/pallas_call | solution.py:536
Async XLA Ops:
  62.7 12.5 %copy-start.2 = (bf16[128,104,128]{2,1,0:T(8,128)(2,1)}, bf16[128,104,128]{2,1,0:T(8,128)(2,1)S(1)}, u32[]{:S(2)}) copy-start(bf16[128,104,128]{2,1,0:T(8,128)(2,1)S(1)} %all_to_all.16.msg_ref.own_ref) | copy-start | bytes 10223620
  62.7 6.6 %collective-permute-start.4 = (bf16[128,104,128]{2,1,0:T(8,128)(2,1)S(1)}, bf16[128,104,128]{2,1,0:T(8,128)(2,1)S(1)}, u32[]{:S(2)}, u32[]{:S(2)}) collective-permute-start(bf16[128,104,128]{2,1,0:T(8,128)(2,1)S(1)} %all_to_all.16.msg_ref.own_ref), channel_id=1, source_target_pairs={{0,4},{1,5},{2,6},{3,7},{4,0},{5,1},{6,2},{7,3},{8,12},{9,13},{10,... | collective-permute-start | bytes 10223624 | tf_op jit(solution)/shard_map/ppermute | solution.py:575
  65.1 4.2 %collective-permute-start.2 = (bf16[272,768]{1,0:T(8,128)(2,1)S(1)}, bf16[272,768]{1,0:T(8,128)(2,1)S(1)}, u32[]{:S(2)}, u32[]{:S(2)}) collective-permute-start(bf16[272,768]{1,0:T(8,128)(2,1)S(1)} %get-tuple-element.75.lone_ref), channel_id=1, source_target_pairs={{0,4},{1,5},{2,6},{3,7},{4,0},{5,1},{6,2},{7,3},{8,12},{9,13},{10,... | collective-permute-start | bytes 1253384 | tf_op jit(solution)/shard_map/ppermute | solution.py:570
  65.4 11.0 %collective-permute-start.3 = (bf16[272,768]{1,0:T(8,128)(2,1)S(1)}, bf16[272,768]{1,0:T(8,128)(2,1)S(1)}, u32[]{:S(2)}, u32[]{:S(2)}) collective-permute-start(bf16[272,768]{1,0:T(8,128)(2,1)S(1)} %get-tuple-element.75.lone_ref), channel_id=1, source_target_pairs={{0,1},{1,0},{2,3},{3,2},{4,5},{5,4},{6,7},{7,6},{8,9},{9,8},{10,11... | collective-permute-start | bytes 1253384 | tf_op jit(solution)/shard_map/ppermute | solution.py:571
  69.4 5.9 %copy-start.3 = (bf16[128,104,128]{2,1,0:T(8,128)(2,1)}, bf16[128,104,128]{2,1,0:T(8,128)(2,1)S(1)}, u32[]{:S(2)}) copy-start(bf16[128,104,128]{2,1,0:T(8,128)(2,1)S(1)} %collective-permute-done.4.other_ref) | copy-start | bytes 10223620
  77.2 14.6 %copy-start = (s32[1024]{0:T(1024)S(1)}, s32[1024]{0:T(1024)}, u32[]{:S(2)}) copy-start(s32[1024]{0:T(1024)} %param.6) | copy-start | bytes 12292
  77.2 14.6 %copy-start.1 = (s32[2,1024]{1,0:T(2,128)S(1)}, s32[2,1024]{1,0:T(2,128)}, u32[]{:S(2)}) copy-start(s32[2,1024]{1,0:T(2,128)} %get-tuple-element.80.index_ref) | copy-start | bytes 24580

commit v3 on v1

--- a/solution.py
+++ b/solution.py
@@ -66,66 +66,82 @@
     return first, second, (left - second.astype(jnp.float32)).astype(jnp.bfloat16)
 
 
-def pack_kernel(emb_ref, cluster_ref, order_ref, out_ref, index_ref, unit_ref, at_ref, some_ref, some_at_ref, late_ref, meta_ref, past_ref):
-    step = pl.program_id(0)
+def pack_kernel(
+    emb_hbm, cluster_hbm, order_hbm, out_hbm, index_ref, out_ref, emb_ref, cluster_ref, order_ref, sems, unit_ref, at_ref,
+    some_ref, some_at_ref, meta_ref, past_ref
+):
     rows = emb_ref.shape[0]
     pairs = PEERS // 2
-    tile = pairs // pl.num_programs(0)
-
-    @pl.when(step == 0)
-    def _():
-        values = emb_ref[...].astype(jnp.float32)
+    steps = 4
+    tile = pairs // steps
+    size = tile * SLOTS
+    chunk = rows // 2
+    spans = [slice(i * chunk, (i + 1) * chunk) for i in range(2)]
+    fetches = [
+        pltpu.make_async_copy(cluster_hbm, cluster_ref, sems.at[4]),
+        pltpu.make_async_copy(order_hbm, order_ref, sems.at[5]),
+    ] + [
+        pltpu.make_async_copy(emb_hbm.at[at, :], emb_ref.at[at, :], sems.at[i])
+        for i, at in enumerate(spans)
+    ]
+    for fetch in fetches:
+        fetch.start()
+    fetches[0].wait()
+    fetches[1].wait()
+    cluster = cluster_ref[...]
+    rank = order_ref[...]
+    hit = iota((CLUSTERS, rows), 0) == cluster
+    hits = ones_where(hit)
+    upper = ones_where(iota((LANES, LANES), 0) <= iota((LANES, LANES), 1))
+    blocks = rows // LANES
+    ahead = dot_nn(hits, ones_where(iota((rows, LANES), 0) >> 7 < iota((rows, LANES), 1)))
+    counted = jnp.concatenate(
+        [
+            dot_nn(hits[:, b * LANES:(b + 1) * LANES], upper) + ahead[:, b:b + 1]
+            for b in range(blocks)
+        ],
+        axis=1,
+    )
+    counts = jnp.broadcast_to(ahead[:, blocks:blocks + 1], (CLUSTERS, LANES))
+    below = ones_where(iota((CLUSTERS, CLUSTERS), 1) < iota((CLUSTERS, CLUSTERS), 0))
+    over = jnp.maximum(counts - 32.0, 0.0)
+    begin = dot_nn(below, over.astype(jnp.bfloat16))
+
+    def of_row(x):
+        return jnp.sum(jnp.where(hit, x, 0.0), axis=0, keepdims=True).astype(jnp.int32)
+
+    index = of_row(counted) - 1
+    count = of_row(counts[:, :1])
+    index_ref[0:1, :] = index
+    index_ref[1:2, :] = count
+    slot = slot_of(index)
+    pair = pair_of(cluster, index)
+    first = index < 32
+    last = index + 32 >= count
+    at_ref[0:1, :] = jnp.where(first, pair * SLOTS + slot, -1)
+    at_ref[1:2, :] = jnp.where(first, -1, of_row(begin[:, :1]) + index - 32)
+    at_ref[2:3, :] = pair
+    at_ref[3:4, :] = slot
+    past_ref[0] = jnp.sum(over[:, :1]).astype(jnp.int32)
+    sends = iota((pairs, rows), 0) == pair
+    sends = jnp.concatenate(
+        [jnp.where(sends & first, 1.0, 0.0), jnp.where(sends & last, 1.0, 0.0)], axis=0
+    )
+    high = ((rank >> 9) + 1).astype(jnp.float32)
+    low = ((rank & 511) - 256).astype(jnp.float32)
+    at_slot = ones_where((iota((LANES, rows), 0) & (SLOTS - 1)) == slot)
+    meta_ref[0] = dot_nt((sends * high).astype(jnp.bfloat16), at_slot)
+    meta_ref[1] = dot_nt((sends * low).astype(jnp.bfloat16), at_slot)
+    spread = jnp.where(iota((CLUSTERS, LANES), 0) == iota((CLUSTERS, LANES), 1), counts, 0.0)
+    meta_ref[2] = jnp.broadcast_to(jnp.sum(spread, axis=0, keepdims=True), (PEERS, LANES))
+    place = iota((PEERS, CLUSTERS), 0) & (pairs - 1)
+    theirs = ones_where((place >> 2) * 2 + (place & 1) == iota((PEERS, CLUSTERS), 1))
+    meta_ref[3] = dot_nn(theirs, counts.astype(jnp.bfloat16))
+    for fetch, at in zip(fetches[2:], spans):
+        fetch.wait()
+        values = emb_ref[at, :].astype(jnp.float32)
         total = jnp.sum(values * values, axis=1, keepdims=True)
-        unit_ref[...] = (values * lax.rsqrt(total + 1e-06)).astype(jnp.bfloat16)
-        cluster = cluster_ref[...]
-        rank = order_ref[...]
-        hit = iota((CLUSTERS, rows), 0) == cluster
-        hits = ones_where(hit)
-        upper = ones_where(iota((LANES, LANES), 0) <= iota((LANES, LANES), 1))
-        blocks = rows // LANES
-        ahead = dot_nn(hits, ones_where(iota((rows, LANES), 0) >> 7 < iota((rows, LANES), 1)))
-        counted = jnp.concatenate(
-            [
-                dot_nn(hits[:, b * LANES:(b + 1) * LANES], upper) + ahead[:, b:b + 1]
-                for b in range(blocks)
-            ],
-            axis=1,
-        )
-        counts = jnp.broadcast_to(ahead[:, blocks:blocks + 1], (CLUSTERS, LANES))
-        below = ones_where(iota((CLUSTERS, CLUSTERS), 1) < iota((CLUSTERS, CLUSTERS), 0))
-        over = jnp.maximum(counts - 32.0, 0.0)
-        begin = dot_nn(below, over.astype(jnp.bfloat16))
-
-        def of_row(x):
-            return jnp.sum(jnp.where(hit, x, 0.0), axis=0, keepdims=True).astype(jnp.int32)
-
-        index = of_row(counted) - 1
-        count = of_row(counts[:, :1])
-        index_ref[0:1, :] = index
-        index_ref[1:2, :] = count
-        slot = slot_of(index)
-        pair = pair_of(cluster, index)
-        first = index < 32
-        last = index + 32 >= count
-        at_ref[0:1, :] = jnp.where(first, pair * SLOTS + slot, -1)
-        at_ref[1:2, :] = jnp.where(first, -1, of_row(begin[:, :1]) + index - 32)
-        at_ref[2:3, :] = pair
-        at_ref[3:4, :] = slot
-        past_ref[0] = jnp.sum(over[:, :1]).astype(jnp.int32)
-        sends = iota((pairs, rows), 0) == pair
-        sends = jnp.concatenate(
-            [jnp.where(sends & first, 1.0, 0.0), jnp.where(sends & last, 1.0, 0.0)], axis=0
-        )
-        high = ((rank >> 9) + 1).astype(jnp.float32)
-        low = ((rank & 511) - 256).astype(jnp.float32)
-        at_slot = ones_where((iota((LANES, rows), 0) & (SLOTS - 1)) == slot)
-        meta_ref[0] = dot_nt((sends * high).astype(jnp.bfloat16), at_slot)
-        meta_ref[1] = dot_nt((sends * low).astype(jnp.bfloat16), at_slot)
-        spread = jnp.where(iota((CLUSTERS, LANES), 0) == iota((CLUSTERS, LANES), 1), counts, 0.0)
-        meta_ref[2] = jnp.broadcast_to(jnp.sum(spread, axis=0, keepdims=True), (PEERS, LANES))
-        place = iota((PEERS, CLUSTERS), 0) & (pairs - 1)
-        theirs = ones_where((place >> 2) * 2 + (place & 1) == iota((PEERS, CLUSTERS), 1))
-        meta_ref[3] = dot_nn(theirs, counts.astype(jnp.bfloat16))
+        unit_ref[at, :] = (values * lax.rsqrt(total + 1e-06)).astype(jnp.bfloat16)
 
     def bring(chunk):
         start = chunk * LANES
@@ -136,77 +152,88 @@
         target = ((place[0:1, :] - 1.0) * SLOTS + place[1:2, :]).astype(jnp.int32)
         some_at_ref[chunk] = jnp.broadcast_to(jnp.where(place[0:1, :] > 0.5, target, -1), (8, LANES))
 
-    @pl.when(step == 0)
-    def _():
-        bring(0)
-
-    size = tile * SLOTS
-    chosen = ones_where(iota((size, rows), 0) + step * size == at_ref[0:1, :])
-    early = dot_nn(chosen, unit_ref[...])
-
-    def spread_some(chunk, late):
+    bring(0)
+
+    def early_rows(step):
+        return dot_nn(ones_where(iota((size, rows), 0) + step * size == at_ref[0:1, :]), unit_ref[...])
+
+    def spread_some(step, chunk, late):
         here = iota((size, LANES), 0) + step * size == some_at_ref[chunk][0:1, :]
         some = dot_nn(ones_where(here), some_ref[chunk * LANES:(chunk + 1) * LANES, :])
         taken = jnp.sum(jnp.where(here, 1.0, 0.0), axis=1, keepdims=True)
         return jnp.where(taken > 0.5, some, late)
 
-    late = spread_some(0, early)
-    start = pl.multiple_of(step * tile, tile)
-
-    def put(half, rows_at):
+    def put(step, half, rows_at):
         packed = rows_at.astype(jnp.bfloat16)
+        peers = pl.ds(step * tile, tile)
         for block in range(BLOCKS):
-            out_ref[:, half, block * SLOTS:(block + 1) * SLOTS, :] = packed[
+            out_ref[peers, half, block * SLOTS:(block + 1) * SLOTS, :] = packed[
                 :, block * LANES:(block + 1) * LANES
             ].reshape(tile, SLOTS, LANES)
 
-    put(0, early)
-    put(1, late)
-    late_ref[...] = late
+    def send(step):
+        peers = pl.ds(step * tile, tile)
+        return pltpu.make_async_copy(out_ref.at[peers], out_hbm.at[peers], sems.at[step])
+
     at = iota((tile, 8, LANES), 1)
-    for half in range(2):
-        meta = jnp.zeros((tile, 8, LANES), jnp.float32)
-        for i in range(4):
-            meta = jnp.where(at == i, meta_ref[i, pl.ds(start + half * pairs, tile), :][:, None, :], meta)
-        out_ref[:, half, DATA:MSG, :] = meta.astype(jnp.bfloat16)
+    for step in range(steps):
+        early = early_rows(step)
+        put(step, 0, early)
+        put(step, 1, spread_some(step, 0, early))
+        for half in range(2):
+            meta = jnp.zeros((tile, 8, LANES), jnp.float32)
+            first = half * pairs + step * tile
+            for i in range(4):
+                meta = jnp.where(at == i, meta_ref[i, first:first + tile, :][:, None, :], meta)
+            out_ref[step * tile:(step + 1) * tile, half, DATA:MSG, :] = meta.astype(jnp.bfloat16)
+        send(step).start()
+    for step in range(steps):
+        send(step).wait()
 
     @pl.when(past_ref[0] > LANES)
     def _():
         for chunk in range(1, rows // LANES // 2):
             bring(chunk)
-            late_ref[...] = spread_some(chunk, late_ref[...])
-        put(1, late_ref[...])
+
+        def again(step, _):
+            late = early_rows(step)
+            for chunk in range(rows // LANES // 2):
+                late = spread_some(step, chunk, late)
+            put(step, 1, late)
+            send(step).start()
+            send(step).wait()
+            return 0
+
+        lax.fori_loop(0, steps, again, 0)
 
 
 def pack(embeddings, cluster, order):
     rows = embeddings.shape[0]
-    steps = 2
     message, index = pl.pallas_call(
         pack_kernel,
-        grid=(steps,),
-        in_specs=[
-            pl.BlockSpec((rows, D), lambda i: (0, 0)),
-            pl.BlockSpec((1, rows), lambda i: (0, 0)),
-            pl.BlockSpec((1, rows), lambda i: (0, 0)),
-        ],
+        in_specs=[pl.BlockSpec(memory_space=pltpu.HBM)] * 3,
         out_specs=[
-            pl.BlockSpec((PEERS // 2 // steps, 2, MSG, LANES), lambda i: (i, 0, 0, 0)),
-            pl.BlockSpec((2, rows), lambda i: (0, 0)),
+            pl.BlockSpec(memory_space=pltpu.HBM),
+            pl.BlockSpec(memory_space=pltpu.VMEM),
         ],
         out_shape=[
             jax.ShapeDtypeStruct((PEERS // 2, 2, MSG, LANES), jnp.bfloat16),
             jax.ShapeDtypeStruct((2, rows), jnp.int32),
         ],
         scratch_shapes=[
+            pltpu.VMEM((PEERS // 2, 2, MSG, LANES), jnp.bfloat16),
+            pltpu.VMEM((rows, D), jnp.bfloat16),
+            pltpu.VMEM((1, rows), jnp.int32),
+            pltpu.VMEM((1, rows), jnp.int32),
+            pltpu.SemaphoreType.DMA((6,)),
             pltpu.VMEM((rows, D), jnp.bfloat16),
             pltpu.VMEM((8, rows), jnp.int32),
             pltpu.VMEM((rows // 2, D), jnp.bfloat16),
             pltpu.VMEM((rows // LANES // 2, 8, LANES), jnp.int32),
-            pltpu.VMEM((rows // steps, D), jnp.float32),
             pltpu.VMEM((4, PEERS, LANES), jnp.float32),
             pltpu.SMEM((1,), jnp.int32),
         ],
-        compiler_params=pltpu.CompilerParams(vmem_limit_bytes=24 * MIB),
+        compiler_params=pltpu.CompilerParams(vmem_limit_bytes=121 * MIB // 2),
         name="pack",
     )(embeddings, cluster.reshape(1, rows), order.reshape(1, rows))
     return message.reshape(PEERS, MSG, LANES), index
@@ -257,14 +284,15 @@
     )
 
 
-def lone_kernel(round_ref, msg_ref, out_ref, most_ref):
+def lone_kernel(round_ref, msg_ref, out_ref, more_ref):
     core = my_core()
     first = 0 if round_ref is None else round_ref[0] * LONE
     held, meta = meta_of(msg_ref)
     high, low, count = (held[:, i:i + 1, :] for i in (0, 1, 3))
     half = jnp.floor((jnp.maximum(meta[:, :, 2, :] - 32.0, 0.0) + 1.0) * 0.5)
     most = jnp.sum(jnp.sum(half, axis=0), axis=0, keepdims=True)
-    most_ref[...] = jnp.max(most, axis=1, keepdims=True).astype(jnp.int32)
+    most = jnp.max(most, axis=1, keepdims=True).astype(jnp.int32)
+    more_ref[...] = (most + LONE - 1) // LONE - 1
 
     index = (2 * (iota((GROUPS, 1, LANES), 2) & 15) + core + 32).astype(jnp.float32)
     lone = jnp.where(index < count, 1.0, 0.0)
@@ -425,6 +453,18 @@
     return jnp.concatenate(parts, axis=0)
 
 
+def placed_by_peer(best, peer, lane):
+    count = best.shape[1]
+    at_peer = ones_where(iota((PEERS, count), 0) == peer)
+    at_lane = iota((HALF, count), 0) == lane
+    first, second, third = (part.astype(jnp.float32) for part in thirds(best))
+    sums = jnp.concatenate([jnp.where(at_lane, part, 0.0) for part in (first, 1.0, second, third)], axis=0)
+    sums = dot_nt(at_peer, sums.astype(jnp.bfloat16))
+    front, back = sums[:, :LANES], sums[:, LANES:]
+    value = front + (back + pltpu.roll(back, HALF, 1))
+    return jnp.where(pltpu.roll(front, HALF, 1) > 0.5, value, -1.0)
+
+
 def finish_kernel(lone_ref, beside_ref, late_ref, best_ref, found_ref, out_ref):
     core, late = my_core(), my_late()
     late_rank, late_peer, late_slot = lone_facts(late_ref)
@@ -456,14 +496,7 @@
     slot = jnp.concatenate(
         [found[0][2] + SLOTS * core, found[1][2] + SLOTS * (1 - core), late_slot + 2 * SLOTS], axis=1
     )
-    at_peer = ones_where(iota((PEERS, 3 * LONE), 0) == peer)
-    at_slot = iota((HALF, 3 * LONE), 0) == slot
-    first, second, third = (part.astype(jnp.float32) for part in thirds(best))
-    sums = jnp.concatenate([jnp.where(at_slot, part, 0.0) for part in (first, 1.0, second, third)], axis=0)
-    sums = dot_nt(at_peer, sums.astype(jnp.bfloat16))
-    front, back = sums[:, :LANES], sums[:, LANES:]
-    value = front + (back + pltpu.roll(back, HALF, 1))
-    table = jnp.where(pltpu.roll(front, HALF, 1) > 0.5, value, -1.0)
+    table = placed_by_peer(best, peer, slot)
     lane = iota((PEERS, LANES), 1)
     rest = jnp.where(
         lane >> 4 == core,
@@ -482,6 +515,41 @@
         compiler_params=pltpu.CompilerParams(vmem_limit_bytes=8 * MIB),
         name="finish",
     )(lone, beside, late_rows, best, found)
+
+
+def rest_kernel(own_ref, other_ref, late_ref, table_ref, out_ref, rank_ref, rows_ref):
+    core = my_core()
+    some = late_ref[:LONE, :]
+    some_rank, peer, slot = lone_facts(late_ref)
+    found = jnp.full((8, LONE), -1.0, jnp.float32)
+    best = []
+    for ref in (own_ref, other_ref):
+        as_columns(ranks_of(ref), rank_ref)
+        for i in range(ROWS // BLOCK):
+            scores = dot_nt(units_of(ref, i * BLOCK, BLOCK), some)
+            rank = wide(rank_ref[span(i), :], LONE)
+            rows_ref[span(i), :] = narrow_rows(jnp.where(some_rank < rank, scores, -1.0))
+            found = jnp.maximum(found, narrow_cols(jnp.where(rank < some_rank, scores, -1.0)))
+        best.append(as_table(row_of_best(rows_ref)))
+    table = placed_by_peer(jnp.max(found, axis=0, keepdims=True), peer, slot + 2 * SLOTS)
+    lane = iota((PEERS, LANES), 1)
+    rest = jnp.where(lane >> 4 == core, best[0], jnp.where(lane < 2 * SLOTS, best[1], table))
+    out_ref[...] = jnp.maximum(table_ref[...], jnp.where(lane < HALF, rest, -1.0))
+
+
+def score_rest(own, other, late_rows, table):
+    return pl.pallas_call(
+        rest_kernel,
+        in_specs=[pl.BlockSpec(memory_space=pltpu.VMEM)] * 4,
+        out_specs=pl.BlockSpec(memory_space=pltpu.VMEM),
+        out_shape=jax.ShapeDtypeStruct((PEERS, LANES), jnp.float32),
+        scratch_shapes=[
+            pltpu.VMEM((ROWS, LANES), jnp.float32),
+            pltpu.VMEM((ROWS, LANES), jnp.float32),
+        ],
+        compiler_params=pltpu.CompilerParams(vmem_limit_bytes=20 * MIB),
+        name="rest",
+    )(own, other, late_rows, table)
 
 
 def reply_kernel(table_ref, cluster_ref, index_ref, out_ref):
@@ -498,6 +566,7 @@
         pltpu.roll(pltpu.roll(table, PEERS - 4, 0), LANES - SLOTS, 1),
     )
     late = jnp.maximum(pltpu.roll(early, PEERS - 1, 0), beside)
+    early = jnp.maximum(early, pltpu.roll(beside, PEERS - 1, 0))
     both = jnp.concatenate([early.T[:2 * SLOTS, :], late.T[:2 * SLOTS, :]], axis=0)
     chosen = ones_where(iota((PEERS, rows), 0) == pair_of(cluster, jnp.zeros_like(index)) * 2)
     picked = dot_nn(jnp.concatenate(thirds(both), axis=0), chosen)
@@ -543,25 +612,23 @@
 def shards(embeddings, cluster, order):
     message, index = pack(embeddings, cluster, order)
     own = lax.all_to_all(message, AXES, split_axis=0, concat_axis=0, tiled=True)
+
     other = lax.ppermute(own, AXES, SWAP)
 
-    def score(lone, far):
+    def score(lone):
         beside = lax.ppermute(lone, AXES, SWAP)
-        far = lax.ppermute(far, AXES, OTHER_CHIP)
+        far = lax.ppermute(lone, AXES, OTHER_CHIP)
         best, found = score_pairs(own, other, lone, beside)
-        return finish(lone, beside, far, best, found)
-
-    lone, most = gather_lone(own)
-    table = score(lone, lone)
-    rounds = (most[0, 0] + LONE - 1) // LONE
+        return far, finish(lone, beside, far, best, found)
 
     def one_round(state):
-        at, table = state
-        lone, _ = gather_lone(own, at // rounds)
-        far, _ = gather_lone(own, at % rounds)
-        return at + 1, jnp.maximum(table, score(lone, far))
-
-    table = lax.while_loop(lambda state: state[0] < rounds * rounds, one_round, (jnp.int32(1), table))[1]
+        left, table = state
+        far, again = score(gather_lone(own, left)[0])
+        return left - 1, score_rest(own, other, far, jnp.maximum(table, again))
+
+    lone, more = gather_lone(own)
+    table = score(lone)[1]
+    table = lax.while_loop(lambda state: state[0] > 0, one_round, (more[0, 0], table))[1]
     replies = lax.all_to_all(table, AXES, split_axis=0, concat_axis=0, tiled=True)
     return read_reply(replies, cluster, index)
 

time: 95 us -> 92.8 us (0.977)
  waiting for transfers between devices: 1.34 us -> 4.82 us
  Pallas kernels: 18.7 us -> 15.8 us
  local copies, waits for them, and re-layouts: 2.79 us -> 0.02 us
    pallas_call x1, Pallas kernels: 8.67 us -> 5.84 us  [score_pairs(): pl.pallas_call(pairs_kernel, in_specs=[vmem] * 4, out_specs=[vmem] * 2, o...]
    unnamed x8, local copies, waits for them, and re-layouts: 2.79 us -> 0.02 us
    ppermute x1, waiting for transfers between devices: 1.06 us -> 3.71 us  [score(): beside = lax.ppermute(lone, AXES, SWAP)]
    pallas_call x1, Pallas kernels: 4.09 us -> 2.11 us  [gather_lone(): pl.pallas_call(lone_kernel if some else functools.partial(lone_kernel, No...]
    pallas_call x1, Pallas kernels: 4.01 us -> 5.91 us  [pack(): pl.pallas_call(pack_kernel, in_specs=[pl.BlockSpec(memory_space=pltpu.HBM...]
  transfers between devices with their start and end apart: 3 -> 3, of which waited for: 2 -> 2; matrix products, arithmetic and copies ran while one was open for 0% -> 0% of each run, Pallas kernels for 13% -> 9%
where the time goes in v3:
time: 92.8 us; the launch traced here: 92.6 us
  blocking collectives  70.4 us (76%)
  Pallas kernels  15.8 us (17%)
  waiting for transfers between devices  4.82 us (5%)
    all_to_all x1, blocking collectives, shards(): own = lax.all_to_all(message, AXES, split_axis=0, concat_axis=0, tiled=True)  56.5 us
    all_to_all x1, blocking collectives, shards(): lax.all_to_all(table, AXES, split_axis=0, concat_axis=0, tiled=True)  13.9 us
    pallas_call x1, Pallas kernels, pack(): pl.pallas_call(pack_kernel, in_specs=[pl.BlockSpec(memory_space=pltpu.HBM...  5.91 us
    pallas_call x1, Pallas kernels, score_pairs(): pl.pallas_call(pairs_kernel, in_specs=[vmem] * 4, out_specs=[vmem] * 2, o...  5.84 us
    ppermute x1, waiting for transfers between devices, score(): beside = lax.ppermute(lone, AXES, SWAP)  3.71 us
    pallas_call x1, Pallas kernels, gather_lone(): pl.pallas_call(lone_kernel if some else functools.partial(lone_kernel, No...  2.11 us
  transfers between devices with their start and end apart: 3, of which 2 were waited for; matrix products, arithmetic and copies ran while one was open for 0% of the time, Pallas kernels for 9%

profile of v3, /device:TPU:1, one launch (start us, length us, event | category | flops | bytes accessed | tf_op | source)
XLA Modules:
  0.0 92.6 jit_solution(6299973757531873566)
XLA Ops:
  0.0 5.9 %pack.1 = (bf16[64,2,104,128]{3,2,1,0:T(8,128)(2,1)}, s32[2,1024]{1,0:T(2,128)}) custom-call(bf16[1024,768]{1,0:T(8,128)(2,1)} %emb_hbm.1, s32[1,1024]{1,0:T(1,128)} %bitcast.11, s32[1,1024]{1,0:T(1,128)} %bitcast.15), custom_call_target="tpu_custom_call" | custom-call | tf_op jit(solution)/shard_map/pack/pallas_call | solution.py:212
  5.9 56.5 %all_to_all.16.msg_ref.own_ref = bf16[128,104,128]{2,1,0:T(8,128)(2,1)S(1)} all-to-all(bf16[128,104,128]{2,1,0:T(8,128)(2,1)} %bitcast.13), channel_id=1, replica_groups=mesh['owner'=32,'split'=4] {'owner','split'}, dimensions={0} | all-to-all | bytes 6815744 | tf_op jit(solution)/shard_map/all_to_all | solution.py:614
  62.5 0.0 copy-start.2
  62.5 0.3 collective-permute-start.4
  62.7 2.1 %lone.5 = (bf16[272,768]{1,0:T(8,128)(2,1)S(1)}, s32[1,1]{1,0:T(1,128)}) custom-call(bf16[128,104,128]{2,1,0:T(8,128)(2,1)S(1)} %all_to_all.16.msg_ref.own_ref), custom_call_target="tpu_custom_call" | custom-call | tf_op jit(solution)/shard_map/lone/pallas_call | solution.py:320
  64.8 0.3 collective-permute-start.2
  65.1 0.3 collective-permute-start.3
  65.4 3.7 %collective-permute-done.2.beside_ref = bf16[272,768]{1,0:T(8,128)(2,1)S(1)} collective-permute-done((bf16[272,768]{1,0:T(8,128)(2,1)S(1)}, bf16[272,768]{1,0:T(8,128)(2,1)S(1)}, u32[]{:S(2)}, u32[]{:S(2)}) %collective-permute-start.2) | collective-permute-done | bytes 417824 | tf_op jit(solution)/shard_map/ppermute | solution.py:619
  69.1 0.0 collective-permute-done.4.other_ref
  69.1 0.0 copy-start.4
  69.1 5.8 %pairs.5 = (f32[2,2048]{1,0:T(2,128)S(1)}, f32[1,256]{1,0:T(1,128)S(1)}) custom-call(bf16[128,104,128]{2,1,0:T(8,128)(2,1)S(1)} %all_to_all.16.msg_ref.own_ref, bf16[128,104,128]{2,1,0:T(8,128)(2,1)S(1)} %collective-permute-done.4.other_ref, bf16[272,768]{1,0:T(8,128)(2,1)S(1)} %get-tuple-element.67.lone_ref, ...), custom_call_target="tpu_custom_call" | custom-call | tf_op jit(solution)/shard_map/pairs/pallas_call | solution.py:426
  75.0 0.0 copy-done.2
  75.0 0.0 copy-done.4
  75.0 1.1 %collective-permute-done.3.late_ref = bf16[272,768]{1,0:T(8,128)(2,1)S(1)} collective-permute-done((bf16[272,768]{1,0:T(8,128)(2,1)S(1)}, bf16[272,768]{1,0:T(8,128)(2,1)S(1)}, u32[]{:S(2)}, u32[]{:S(2)}) %collective-permute-start.3) | collective-permute-done | bytes 417824 | tf_op jit(solution)/shard_map/ppermute | solution.py:620
  76.1 0.9 finish.5
  76.9 0.0 copy-start
  77.0 0.0 copy-start.1
  77.0 0.7 while.12
  77.6 13.9 %all_to_all.17 = f32[128,1,128]{2,1,0:T(1,128)S(1)} all-to-all(f32[128,1,128]{2,1,0:T(1,128)S(1)} %bitcast.14), channel_id=1, replica_groups=mesh['owner'=32,'split'=4] {'owner','split'}, dimensions={0} | all-to-all | bytes 131072 | tf_op jit(solution)/shard_map/all_to_all | solution.py:632
  91.5 0.0 copy-done
  91.5 0.0 copy-done.1
  91.5 1.1 %reply.1 = f32[1,1024]{1,0:T(1,128)} custom-call(f32[128,128]{1,0:T(8,128)S(1)} %bitcast.10, s32[1,1024]{1,0:T(1,128)S(1)} %bitcast.12, s32[2,1024]{1,0:T(2,128)S(1)} %copy-done.1), custom_call_target="tpu_custom_call" | custom-call | tf_op jit(solution)/shard_map/reply/pallas_call | solution.py:583
Async XLA Ops:
  62.5 12.5 %copy-start.2 = (bf16[128,104,128]{2,1,0:T(8,128)(2,1)}, bf16[128,104,128]{2,1,0:T(8,128)(2,1)S(1)}, u32[]{:S(2)}) copy-start(bf16[128,104,128]{2,1,0:T(8,128)(2,1)S(1)} %all_to_all.16.msg_ref.own_ref) | copy-start | bytes 10223620
  62.5 6.6 %collective-permute-start.4 = (bf16[128,104,128]{2,1,0:T(8,128)(2,1)S(1)}, bf16[128,104,128]{2,1,0:T(8,128)(2,1)S(1)}, u32[]{:S(2)}, u32[]{:S(2)}) collective-permute-start(bf16[128,104,128]{2,1,0:T(8,128)(2,1)S(1)} %all_to_all.16.msg_ref.own_ref), channel_id=1, source_target_pairs={{0,4},{1,5},{2,6},{3,7},{4,0},{5,1},{6,2},{7,3},{8,12},{9,13},{10,... | collective-permute-start | bytes 10223624 | tf_op jit(solution)/shard_map/ppermute | solution.py:616
  64.8 4.3 %collective-permute-start.2 = (bf16[272,768]{1,0:T(8,128)(2,1)S(1)}, bf16[272,768]{1,0:T(8,128)(2,1)S(1)}, u32[]{:S(2)}, u32[]{:S(2)}) collective-permute-start(bf16[272,768]{1,0:T(8,128)(2,1)S(1)} %get-tuple-element.67.lone_ref), channel_id=1, source_target_pairs={{0,4},{1,5},{2,6},{3,7},{4,0},{5,1},{6,2},{7,3},{8,12},{9,13},{10,... | collective-permute-start | bytes 1253384 | tf_op jit(solution)/shard_map/ppermute | solution.py:619
  65.1 11.0 %collective-permute-start.3 = (bf16[272,768]{1,0:T(8,128)(2,1)S(1)}, bf16[272,768]{1,0:T(8,128)(2,1)S(1)}, u32[]{:S(2)}, u32[]{:S(2)}) collective-permute-start(bf16[272,768]{1,0:T(8,128)(2,1)S(1)} %get-tuple-element.67.lone_ref), channel_id=1, source_target_pairs={{0,1},{1,0},{2,3},{3,2},{4,5},{5,4},{6,7},{7,6},{8,9},{9,8},{10,11... | collective-permute-start | bytes 1253384 | tf_op jit(solution)/shard_map/ppermute | solution.py:620
  69.1 5.9 %copy-start.4 = (bf16[128,104,128]{2,1,0:T(8,128)(2,1)}, bf16[128,104,128]{2,1,0:T(8,128)(2,1)S(1)}, u32[]{:S(2)}) copy-start(bf16[128,104,128]{2,1,0:T(8,128)(2,1)S(1)} %collective-permute-done.4.other_ref) | copy-start | bytes 10223620
  76.9 14.6 %copy-start = (s32[1024]{0:T(1024)S(1)}, s32[1024]{0:T(1024)}, u32[]{:S(2)}) copy-start(s32[1024]{0:T(1024)} %param.6) | copy-start | bytes 12292
  77.0 14.5 %copy-start.1 = (s32[2,1024]{1,0:T(2,128)S(1)}, s32[2,1024]{1,0:T(2,128)}, u32[]{:S(2)}) copy-start(s32[2,1024]{1,0:T(2,128)} %get-tuple-element.71.index_ref) | copy-start | bytes 24580

commit v4 on v3

--- a/solution.py
+++ b/solution.py
@@ -78,10 +78,10 @@
     chunk = rows // 2
     spans = [slice(i * chunk, (i + 1) * chunk) for i in range(2)]
     fetches = [
-        pltpu.make_async_copy(cluster_hbm, cluster_ref, sems.at[4]),
-        pltpu.make_async_copy(order_hbm, order_ref, sems.at[5]),
+        pltpu.make_async_copy(cluster_hbm, cluster_ref, sems.at[0, 0]),
+        pltpu.make_async_copy(order_hbm, order_ref, sems.at[0, 1]),
     ] + [
-        pltpu.make_async_copy(emb_hbm.at[at, :], emb_ref.at[at, :], sems.at[i])
+        pltpu.make_async_copy(emb_hbm.at[at, :], emb_ref.at[at, :], sems.at[1, i])
         for i, at in enumerate(spans)
     ]
     for fetch in fetches:
@@ -152,8 +152,6 @@
         target = ((place[0:1, :] - 1.0) * SLOTS + place[1:2, :]).astype(jnp.int32)
         some_at_ref[chunk] = jnp.broadcast_to(jnp.where(place[0:1, :] > 0.5, target, -1), (8, LANES))
 
-    bring(0)
-
     def early_rows(step):
         return dot_nn(ones_where(iota((size, rows), 0) + step * size == at_ref[0:1, :]), unit_ref[...])
 
@@ -171,24 +169,32 @@
                 :, block * LANES:(block + 1) * LANES
             ].reshape(tile, SLOTS, LANES)
 
-    def send(step):
+    def send(step, half):
         peers = pl.ds(step * tile, tile)
-        return pltpu.make_async_copy(out_ref.at[peers], out_hbm.at[peers], sems.at[step])
+        return pltpu.make_async_copy(out_ref.at[peers, half], out_hbm.at[peers, half], sems.at[half, step])
 
     at = iota((tile, 8, LANES), 1)
+
+    def finish_tile(step, half, rows_at):
+        put(step, half, rows_at)
+        meta = jnp.zeros((tile, 8, LANES), jnp.float32)
+        first = half * pairs + step * tile
+        for i in range(4):
+            meta = jnp.where(at == i, meta_ref[i, first:first + tile, :][:, None, :], meta)
+        out_ref[step * tile:(step + 1) * tile, half, DATA:MSG, :] = meta.astype(jnp.bfloat16)
+        send(step, half).start()
+
+    early = []
     for step in range(steps):
-        early = early_rows(step)
-        put(step, 0, early)
-        put(step, 1, spread_some(step, 0, early))
-        for half in range(2):
-            meta = jnp.zeros((tile, 8, LANES), jnp.float32)
-            first = half * pairs + step * tile
-            for i in range(4):
-                meta = jnp.where(at == i, meta_ref[i, first:first + tile, :][:, None, :], meta)
-            out_ref[step * tile:(step + 1) * tile, half, DATA:MSG, :] = meta.astype(jnp.bfloat16)
-        send(step).start()
+        early.append(early_rows(step))
+        finish_tile(step, 0, early[step])
+        if step == 1:
+            bring(0)
     for step in range(steps):
-        send(step).wait()
+        finish_tile(step, 1, spread_some(step, 0, early[step]))
+    for half in range(2):
+        for step in range(steps):
+            send(step, half).wait()
 
     @pl.when(past_ref[0] > LANES)
     def _():
@@ -200,8 +206,8 @@
             for chunk in range(rows // LANES // 2):
                 late = spread_some(step, chunk, late)
             put(step, 1, late)
-            send(step).start()
-            send(step).wait()
+            send(step, 1).start()
+            send(step, 1).wait()
             return 0
 
         lax.fori_loop(0, steps, again, 0)
@@ -225,7 +231,7 @@
             pltpu.VMEM((rows, D), jnp.bfloat16),
             pltpu.VMEM((1, rows), jnp.int32),
             pltpu.VMEM((1, rows), jnp.int32),
-            pltpu.SemaphoreType.DMA((6,)),
+            pltpu.SemaphoreType.DMA((2, 4)),
             pltpu.VMEM((rows, D), jnp.bfloat16),
             pltpu.VMEM((8, rows), jnp.int32),
             pltpu.VMEM((rows // 2, D), jnp.bfloat16),
@@ -474,13 +480,13 @@
     )
     late_column = wide(late_column, LONE)
     late_best = jnp.full((LONE, LANES), -1.0, jnp.float32)
-    found = []
-    for ref in (lone_ref, beside_ref):
-        rank, peer, slot = lone_facts(ref)
-        scores = dot_nt(late_ref[:LONE, :], ref[:LONE, :])
-        late_best = jnp.maximum(late_best, narrow_rows(jnp.where(rank < late_column, scores, -1.0)))
-        best = jnp.max(jnp.where(late_column < rank, scores, -1.0), axis=0, keepdims=True)
-        found.append((best, peer, slot))
+    _, own_peer, own_slot = lone_facts(lone_ref)
+    _, other_peer, other_slot = lone_facts(beside_ref)
+    facts = jnp.where(late == 0, lone_ref[LONE:, :], beside_ref[LONE:, :])[:, :LONE].astype(jnp.float32)
+    rank = rank_from(facts[0:1, :], facts[1:2, :])
+    scores = dot_nt(late_ref[:LONE, :], jnp.where(late == 0, lone_ref[:LONE, :], beside_ref[:LONE, :]))
+    late_best = jnp.maximum(late_best, narrow_rows(jnp.where(rank < late_column, scores, -1.0)))
+    seen = jnp.max(jnp.where(late_column < rank, scores, -1.0), axis=0, keepdims=True)
     late_best = jnp.concatenate(
         [
             jnp.max(late_best[b * LANES:(b + 1) * LANES, :].T, axis=0, keepdims=True)
@@ -489,12 +495,12 @@
         axis=1,
     )
     earlier_found = found_ref[...]
-    own = jnp.maximum(found[0][0], jnp.where(late == 1, earlier_found, -1.0))
-    other = jnp.maximum(found[1][0], jnp.where(late == 0, earlier_found, -1.0))
+    own = jnp.where(late == 0, seen, earlier_found)
+    other = jnp.where(late == 0, earlier_found, seen)
     best = jnp.concatenate([own, other, late_best], axis=1)
-    peer = jnp.concatenate([found[0][1], found[1][1], late_peer], axis=1)
+    peer = jnp.concatenate([own_peer, other_peer, late_peer], axis=1)
     slot = jnp.concatenate(
-        [found[0][2] + SLOTS * core, found[1][2] + SLOTS * (1 - core), late_slot + 2 * SLOTS], axis=1
+        [own_slot + SLOTS * core, other_slot + SLOTS * (1 - core), late_slot + 2 * SLOTS], axis=1
     )
     table = placed_by_peer(best, peer, slot)
     lane = iota((PEERS, LANES), 1)
@@ -623,12 +629,12 @@
 
     def one_round(state):
         left, table = state
-        far, again = score(gather_lone(own, left)[0])
+        far, again = score(gather_lone(own, left[0, 0])[0])
         return left - 1, score_rest(own, other, far, jnp.maximum(table, again))
 
     lone, more = gather_lone(own)
     table = score(lone)[1]
-    table = lax.while_loop(lambda state: state[0] > 0, one_round, (more[0, 0], table))[1]
+    table = lax.while_loop(lambda state: state[0][0, 0] > 0, one_round, (more, table))[1]
     replies = lax.all_to_all(table, AXES, split_axis=0, concat_axis=0, tiled=True)
     return read_reply(replies, cluster, index)
 

time: 92.8 us -> 92.8 us (level)
  no operation moved by 1% of the time
where the time goes in v4:
time: 92.8 us; the launch traced here: 92.5 us
  blocking collectives  70.4 us (76%)
  Pallas kernels  15.7 us (17%)
  waiting for transfers between devices  4.86 us (5%)
    all_to_all x1, blocking collectives, shards(): own = lax.all_to_all(message, AXES, split_axis=0, concat_axis=0, tiled=True)  56.5 us
    all_to_all x1, blocking collectives, shards(): lax.all_to_all(table, AXES, split_axis=0, concat_axis=0, tiled=True)  13.9 us
    pallas_call x1, Pallas kernels, pack(): pl.pallas_call(pack_kernel, in_specs=[pl.BlockSpec(memory_space=pltpu.HBM...  5.9 us
    pallas_call x1, Pallas kernels, score_pairs(): pl.pallas_call(pairs_kernel, in_specs=[vmem] * 4, out_specs=[vmem] * 2, o...  5.82 us
    ppermute x1, waiting for transfers between devices, score(): beside = lax.ppermute(lone, AXES, SWAP)  3.72 us
    pallas_call x1, Pallas kernels, gather_lone(): pl.pallas_call(lone_kernel if some else functools.partial(lone_kernel, No...  2.1 us
  transfers between devices with their start and end apart: 3, of which 2 were waited for; matrix products, arithmetic and copies ran while one was open for 0% of the time, Pallas kernels for 9%

profile of v4, /device:TPU:1, one launch (start us, length us, event | category | flops | bytes accessed | tf_op | source)
XLA Modules:
  0.0 92.5 jit_solution(15382635044724970659)
XLA Ops:
  0.0 5.9 %pack.1 = (bf16[64,2,104,128]{3,2,1,0:T(8,128)(2,1)}, s32[2,1024]{1,0:T(2,128)}) custom-call(bf16[1024,768]{1,0:T(8,128)(2,1)} %emb_hbm.1, s32[1,1024]{1,0:T(1,128)} %bitcast.11, s32[1,1024]{1,0:T(1,128)} %bitcast.15), custom_call_target="tpu_custom_call" | custom-call | tf_op jit(solution)/shard_map/pack/pallas_call | solution.py:218
  5.9 56.5 %all_to_all.16.msg_ref.own_ref = bf16[128,104,128]{2,1,0:T(8,128)(2,1)S(1)} all-to-all(bf16[128,104,128]{2,1,0:T(8,128)(2,1)} %bitcast.13), channel_id=1, replica_groups=mesh['owner'=32,'split'=4] {'owner','split'}, dimensions={0} | all-to-all | bytes 6815744 | tf_op jit(solution)/shard_map/all_to_all | solution.py:620
  62.5 0.3 collective-permute-start.4
  62.7 2.1 %lone.5 = (bf16[272,768]{1,0:T(8,128)(2,1)S(1)}, s32[1,1]{1,0:T(1,128)}) custom-call(bf16[128,104,128]{2,1,0:T(8,128)(2,1)S(1)} %all_to_all.16.msg_ref.own_ref), custom_call_target="tpu_custom_call" | custom-call | tf_op jit(solution)/shard_map/lone/pallas_call | solution.py:326
  64.8 0.3 collective-permute-start.2
  65.1 0.3 collective-permute-start.3
  65.4 3.7 %collective-permute-done.2.beside_ref = bf16[272,768]{1,0:T(8,128)(2,1)S(1)} collective-permute-done((bf16[272,768]{1,0:T(8,128)(2,1)S(1)}, bf16[272,768]{1,0:T(8,128)(2,1)S(1)}, u32[]{:S(2)}, u32[]{:S(2)}) %collective-permute-start.2) | collective-permute-done | bytes 417824 | tf_op jit(solution)/shard_map/ppermute | solution.py:625
  69.1 0.0 collective-permute-done.4.other_ref
  69.1 5.8 %pairs.5 = (f32[2,2048]{1,0:T(2,128)S(1)}, f32[1,256]{1,0:T(1,128)S(1)}) custom-call(bf16[128,104,128]{2,1,0:T(8,128)(2,1)S(1)} %all_to_all.16.msg_ref.own_ref, bf16[128,104,128]{2,1,0:T(8,128)(2,1)S(1)} %collective-permute-done.4.other_ref, bf16[272,768]{1,0:T(8,128)(2,1)S(1)} %get-tuple-element.67.lone_ref, ...), custom_call_target="tpu_custom_call" | custom-call | tf_op jit(solution)/shard_map/pairs/pallas_call | solution.py:432
  74.9 1.1 %collective-permute-done.3.late_ref = bf16[272,768]{1,0:T(8,128)(2,1)S(1)} collective-permute-done((bf16[272,768]{1,0:T(8,128)(2,1)S(1)}, bf16[272,768]{1,0:T(8,128)(2,1)S(1)}, u32[]{:S(2)}, u32[]{:S(2)}) %collective-permute-start.3) | collective-permute-done | bytes 417824 | tf_op jit(solution)/shard_map/ppermute | solution.py:626
  76.1 0.8 finish.5
  76.9 0.0 copy-start
  76.9 0.0 copy-start.1
  76.9 0.7 while.12
  77.6 13.9 %all_to_all.17 = f32[128,1,128]{2,1,0:T(1,128)S(1)} all-to-all(f32[128,1,128]{2,1,0:T(1,128)S(1)} %bitcast.14), channel_id=1, replica_groups=mesh['owner'=32,'split'=4] {'owner','split'}, dimensions={0} | all-to-all | bytes 131072 | tf_op jit(solution)/shard_map/all_to_all | solution.py:638
  91.5 0.0 copy-done
  91.5 0.0 copy-done.1
  91.5 1.1 %reply.1 = f32[1,1024]{1,0:T(1,128)} custom-call(f32[128,128]{1,0:T(8,128)S(1)} %bitcast.10, s32[1,1024]{1,0:T(1,128)S(1)} %bitcast.12, s32[2,1024]{1,0:T(2,128)S(1)} %copy-done.1), custom_call_target="tpu_custom_call" | custom-call | tf_op jit(solution)/shard_map/reply/pallas_call | solution.py:589
Async XLA Ops:
  62.5 6.6 %collective-permute-start.4 = (bf16[128,104,128]{2,1,0:T(8,128)(2,1)S(1)}, bf16[128,104,128]{2,1,0:T(8,128)(2,1)S(1)}, u32[]{:S(2)}, u32[]{:S(2)}) collective-permute-start(bf16[128,104,128]{2,1,0:T(8,128)(2,1)S(1)} %all_to_all.16.msg_ref.own_ref), channel_id=1, source_target_pairs={{0,4},{1,5},{2,6},{3,7},{4,0},{5,1},{6,2},{7,3},{8,12},{9,13},{10,... | collective-permute-start | bytes 10223624 | tf_op jit(solution)/shard_map/ppermute | solution.py:622
  64.8 4.3 %collective-permute-start.2 = (bf16[272,768]{1,0:T(8,128)(2,1)S(1)}, bf16[272,768]{1,0:T(8,128)(2,1)S(1)}, u32[]{:S(2)}, u32[]{:S(2)}) collective-permute-start(bf16[272,768]{1,0:T(8,128)(2,1)S(1)} %get-tuple-element.67.lone_ref), channel_id=1, source_target_pairs={{0,4},{1,5},{2,6},{3,7},{4,0},{5,1},{6,2},{7,3},{8,12},{9,13},{10,... | collective-permute-start | bytes 1253384 | tf_op jit(solution)/shard_map/ppermute | solution.py:625
  65.1 11.0 %collective-permute-start.3 = (bf16[272,768]{1,0:T(8,128)(2,1)S(1)}, bf16[272,768]{1,0:T(8,128)(2,1)S(1)}, u32[]{:S(2)}, u32[]{:S(2)}) collective-permute-start(bf16[272,768]{1,0:T(8,128)(2,1)S(1)} %get-tuple-element.67.lone_ref), channel_id=1, source_target_pairs={{0,1},{1,0},{2,3},{3,2},{4,5},{5,4},{6,7},{7,6},{8,9},{9,8},{10,11... | collective-permute-start | bytes 1253384 | tf_op jit(solution)/shard_map/ppermute | solution.py:626
  76.9 14.6 %copy-start = (s32[1024]{0:T(1024)S(1)}, s32[1024]{0:T(1024)}, u32[]{:S(2)}) copy-start(s32[1024]{0:T(1024)} %param.6) | copy-start | bytes 12292
  76.9 14.6 %copy-start.1 = (s32[2,1024]{1,0:T(2,128)S(1)}, s32[2,1024]{1,0:T(2,128)}, u32[]{:S(2)}) copy-start(s32[2,1024]{1,0:T(2,128)} %get-tuple-element.71.index_ref) | copy-start | bytes 24580

commit v5 on v3

--- a/solution.py
+++ b/solution.py
@@ -72,7 +72,7 @@
 ):
     rows = emb_ref.shape[0]
     pairs = PEERS // 2
-    steps = 4
+    steps = 8
     tile = pairs // steps
     size = tile * SLOTS
     chunk = rows // 2
@@ -225,7 +225,7 @@
             pltpu.VMEM((rows, D), jnp.bfloat16),
             pltpu.VMEM((1, rows), jnp.int32),
             pltpu.VMEM((1, rows), jnp.int32),
-            pltpu.SemaphoreType.DMA((6,)),
+            pltpu.SemaphoreType.DMA((8,)),
             pltpu.VMEM((rows, D), jnp.bfloat16),
             pltpu.VMEM((8, rows), jnp.int32),
             pltpu.VMEM((rows // 2, D), jnp.bfloat16),

time: 92.8 us -> 92.8 us (level)
  no operation moved by 1% of the time
where the time goes in v5:
time: 92.8 us; the launch traced here: 92.5 us
  blocking collectives  70.4 us (76%)
  Pallas kernels  15.8 us (17%)
  waiting for transfers between devices  4.8 us (5%)
    all_to_all x1, blocking collectives, shards(): own = lax.all_to_all(message, AXES, split_axis=0, concat_axis=0, tiled=True)  56.6 us
    all_to_all x1, blocking collectives, shards(): lax.all_to_all(table, AXES, split_axis=0, concat_axis=0, tiled=True)  13.9 us
    pallas_call x1, Pallas kernels, score_pairs(): pl.pallas_call(pairs_kernel, in_specs=[vmem] * 4, out_specs=[vmem] * 2, o...  5.87 us
    pallas_call x1, Pallas kernels, pack(): pl.pallas_call(pack_kernel, in_specs=[pl.BlockSpec(memory_space=pltpu.HBM...  5.86 us
    ppermute x1, waiting for transfers between devices, score(): beside = lax.ppermute(lone, AXES, SWAP)  3.71 us
    pallas_call x1, Pallas kernels, gather_lone(): pl.pallas_call(lone_kernel if some else functools.partial(lone_kernel, No...  2.11 us
  transfers between devices with their start and end apart: 3, of which 2 were waited for; matrix products, arithmetic and copies ran while one was open for 0% of the time, Pallas kernels for 9%

profile of v5, /device:TPU:1, one launch (start us, length us, event | category | flops | bytes accessed | tf_op | source)
XLA Modules:
  0.0 92.5 jit_solution(15951441583119124249)
XLA Ops:
  0.0 5.9 %pack.1 = (bf16[64,2,104,128]{3,2,1,0:T(8,128)(2,1)}, s32[2,1024]{1,0:T(2,128)}) custom-call(bf16[1024,768]{1,0:T(8,128)(2,1)} %emb_hbm.1, s32[1,1024]{1,0:T(1,128)} %bitcast.11, s32[1,1024]{1,0:T(1,128)} %bitcast.15), custom_call_target="tpu_custom_call" | custom-call | tf_op jit(solution)/shard_map/pack/pallas_call | solution.py:212
  5.9 56.6 %all_to_all.16.msg_ref.own_ref = bf16[128,104,128]{2,1,0:T(8,128)(2,1)S(1)} all-to-all(bf16[128,104,128]{2,1,0:T(8,128)(2,1)} %bitcast.13), channel_id=1, replica_groups=mesh['owner'=32,'split'=4] {'owner','split'}, dimensions={0} | all-to-all | bytes 6815744 | tf_op jit(solution)/shard_map/all_to_all | solution.py:614
  62.4 0.0 copy-start.2
  62.4 0.3 collective-permute-start.4
  62.7 2.1 %lone.5 = (bf16[272,768]{1,0:T(8,128)(2,1)S(1)}, s32[1,1]{1,0:T(1,128)}) custom-call(bf16[128,104,128]{2,1,0:T(8,128)(2,1)S(1)} %all_to_all.16.msg_ref.own_ref), custom_call_target="tpu_custom_call" | custom-call | tf_op jit(solution)/shard_map/lone/pallas_call | solution.py:320
  64.8 0.3 collective-permute-start.2
  65.0 0.3 collective-permute-start.3
  65.4 3.7 %collective-permute-done.2.beside_ref = bf16[272,768]{1,0:T(8,128)(2,1)S(1)} collective-permute-done((bf16[272,768]{1,0:T(8,128)(2,1)S(1)}, bf16[272,768]{1,0:T(8,128)(2,1)S(1)}, u32[]{:S(2)}, u32[]{:S(2)}) %collective-permute-start.2) | collective-permute-done | bytes 417824 | tf_op jit(solution)/shard_map/ppermute | solution.py:619
  69.1 0.0 collective-permute-done.4.other_ref
  69.1 0.0 copy-start.4
  69.1 5.9 %pairs.5 = (f32[2,2048]{1,0:T(2,128)S(1)}, f32[1,256]{1,0:T(1,128)S(1)}) custom-call(bf16[128,104,128]{2,1,0:T(8,128)(2,1)S(1)} %all_to_all.16.msg_ref.own_ref, bf16[128,104,128]{2,1,0:T(8,128)(2,1)S(1)} %collective-permute-done.4.other_ref, bf16[272,768]{1,0:T(8,128)(2,1)S(1)} %get-tuple-element.67.lone_ref, ...), custom_call_target="tpu_custom_call" | custom-call | tf_op jit(solution)/shard_map/pairs/pallas_call | solution.py:426
  74.9 0.0 copy-done.2
  75.0 0.0 copy-done.4
  75.0 1.1 %collective-permute-done.3.late_ref = bf16[272,768]{1,0:T(8,128)(2,1)S(1)} collective-permute-done((bf16[272,768]{1,0:T(8,128)(2,1)S(1)}, bf16[272,768]{1,0:T(8,128)(2,1)S(1)}, u32[]{:S(2)}, u32[]{:S(2)}) %collective-permute-start.3) | collective-permute-done | bytes 417824 | tf_op jit(solution)/shard_map/ppermute | solution.py:620
  76.0 0.9 finish.5
  76.9 0.0 copy-start
  76.9 0.0 copy-start.1
  76.9 0.7 while.12
  77.6 13.9 %all_to_all.17 = f32[128,1,128]{2,1,0:T(1,128)S(1)} all-to-all(f32[128,1,128]{2,1,0:T(1,128)S(1)} %bitcast.14), channel_id=1, replica_groups=mesh['owner'=32,'split'=4] {'owner','split'}, dimensions={0} | all-to-all | bytes 131072 | tf_op jit(solution)/shard_map/all_to_all | solution.py:632
  91.5 0.0 copy-done
  91.5 0.0 copy-done.1
  91.5 1.1 %reply.1 = f32[1,1024]{1,0:T(1,128)} custom-call(f32[128,128]{1,0:T(8,128)S(1)} %bitcast.10, s32[1,1024]{1,0:T(1,128)S(1)} %bitcast.12, s32[2,1024]{1,0:T(2,128)S(1)} %copy-done.1), custom_call_target="tpu_custom_call" | custom-call | tf_op jit(solution)/shard_map/reply/pallas_call | solution.py:583
Async XLA Ops:
  62.4 12.5 %copy-start.2 = (bf16[128,104,128]{2,1,0:T(8,128)(2,1)}, bf16[128,104,128]{2,1,0:T(8,128)(2,1)S(1)}, u32[]{:S(2)}) copy-start(bf16[128,104,128]{2,1,0:T(8,128)(2,1)S(1)} %all_to_all.16.msg_ref.own_ref) | copy-start | bytes 10223620
  62.4 6.6 %collective-permute-start.4 = (bf16[128,104,128]{2,1,0:T(8,128)(2,1)S(1)}, bf16[128,104,128]{2,1,0:T(8,128)(2,1)S(1)}, u32[]{:S(2)}, u32[]{:S(2)}) collective-permute-start(bf16[128,104,128]{2,1,0:T(8,128)(2,1)S(1)} %all_to_all.16.msg_ref.own_ref), channel_id=1, source_target_pairs={{0,4},{1,5},{2,6},{3,7},{4,0},{5,1},{6,2},{7,3},{8,12},{9,13},{10,... | collective-permute-start | bytes 10223624 | tf_op jit(solution)/shard_map/ppermute | solution.py:616
  64.8 4.3 %collective-permute-start.2 = (bf16[272,768]{1,0:T(8,128)(2,1)S(1)}, bf16[272,768]{1,0:T(8,128)(2,1)S(1)}, u32[]{:S(2)}, u32[]{:S(2)}) collective-permute-start(bf16[272,768]{1,0:T(8,128)(2,1)S(1)} %get-tuple-element.67.lone_ref), channel_id=1, source_target_pairs={{0,4},{1,5},{2,6},{3,7},{4,0},{5,1},{6,2},{7,3},{8,12},{9,13},{10,... | collective-permute-start | bytes 1253384 | tf_op jit(solution)/shard_map/ppermute | solution.py:619
  65.0 11.0 %collective-permute-start.3 = (bf16[272,768]{1,0:T(8,128)(2,1)S(1)}, bf16[272,768]{1,0:T(8,128)(2,1)S(1)}, u32[]{:S(2)}, u32[]{:S(2)}) collective-permute-start(bf16[272,768]{1,0:T(8,128)(2,1)S(1)} %get-tuple-element.67.lone_ref), channel_id=1, source_target_pairs={{0,1},{1,0},{2,3},{3,2},{4,5},{5,4},{6,7},{7,6},{8,9},{9,8},{10,11... | collective-permute-start | bytes 1253384 | tf_op jit(solution)/shard_map/ppermute | solution.py:620
  69.1 5.9 %copy-start.4 = (bf16[128,104,128]{2,1,0:T(8,128)(2,1)}, bf16[128,104,128]{2,1,0:T(8,128)(2,1)S(1)}, u32[]{:S(2)}) copy-start(bf16[128,104,128]{2,1,0:T(8,128)(2,1)S(1)} %collective-permute-done.4.other_ref) | copy-start | bytes 10223620
  76.9 14.6 %copy-start = (s32[1024]{0:T(1024)S(1)}, s32[1024]{0:T(1024)}, u32[]{:S(2)}) copy-start(s32[1024]{0:T(1024)} %param.6) | copy-start | bytes 12292
  76.9 14.6 %copy-start.1 = (s32[2,1024]{1,0:T(2,128)S(1)}, s32[2,1024]{1,0:T(2,128)}, u32[]{:S(2)}) copy-start(s32[2,1024]{1,0:T(2,128)} %get-tuple-element.71.index_ref) | copy-start | bytes 24580
